TPU v7x, 32 devices: a whole 2x2x4 slice. The times are simulated.
32 devices in a mesh: dp: 4 (over y, x), tensor: 8 (over z, core).
Axes of the slice: x: 2, y: 2, z: 4, core: 2. Of those that a mesh axis runs over, the one named last changes fastest.
Arguments:
- tokens: bfloat16 [2048, 3584], P(('dp', 'tensor')), may hold values from -6 to 6
- cotangent: bfloat16 [2048, 3584], P(('dp', 'tensor')), may hold values from -6 to 6
- gate_weight: bfloat16 [3584, 10240], P(None, 'tensor'), may hold values from -0.09375 to 0.09375
- up_weight: bfloat16 [3584, 10240], P(None, 'tensor'), may hold values from -0.09375 to 0.09375
- down_weight: bfloat16 [10240, 3584], P('tensor'), may hold values from -0.0625 to 0.0625
- adapter_first_factors: bfloat16 [3584, 128], replicated, may hold values from -0.09375 to 0.09375
- adapter_second_factors: bfloat16 [2, 64, 10240], P(None, None, 'tensor'), may hold values from -0.75 to 0.75
- down_factor_first: bfloat16 [64, 10240], P(None, 'tensor'), may hold values from -0.0625 to 0.0625
- down_factor_second: bfloat16 [64, 3584], replicated, may hold values from -0.75 to 0.75
Outputs:
- input_gradient: bfloat16 [2048, 3584], P(('dp', 'tensor'))
- adapter_first_gradient: float32 [3584, 128], replicated
- adapter_second_gradient: float32 [2, 64, 10240], P(None, None, 'tensor')
- down_first_gradient: float32 [64, 10240], P(None, 'tensor')
- down_second_gradient: float32 [64, 3584], replicated
All inputs are finite; a program needn't handle non-finite values.
Results may differ from a plain program's by a relative error of at most 0.017.
Values may be sent and summed in bfloat16 or wider, within the bound.
A program may use at most 128 MiB of HBM per device.

v0:
```python
import math

import jax
import jax.numpy as jnp
from jax import lax
from jax.sharding import PartitionSpec as P

adapter_scale = 0.5


def contraction_rows(left, right):
    return lax.dot_general(
        left, right, (((0,), (0,)), ((), ())), preferred_element_type=jnp.float32
    )


def contract_columns(left, right):
    return lax.dot_general(
        left, right, (((1,), (1,)), ((), ())), preferred_element_type=jnp.float32
    )


def exact_rows(left, right):
    return lax.dot_general(
        left.astype(jnp.float32),
        right.astype(jnp.float32),
        (((0,), (0,)), ((), ())),
        precision=lax.Precision.HIGHEST,
        preferred_element_type=jnp.float32,
    )


def exact_columns(left, right):
    return lax.dot_general(
        left,
        right.astype(jnp.float32),
        (((1,), (1,)), ((), ())),
        precision=lax.Precision.HIGHEST,
        preferred_element_type=jnp.float32,
    )


def shards(
    tokens,
    cotangent,
    gate_weight,
    up_weight,
    down_weight,
    adapter_first_factors,
    adapter_second_factors,
    down_factor_first,
    down_factor_second,
):
    tok_rows = tokens.shape[0]
    rank_count = adapter_second_factors.shape[1]
    token_total = tok_rows * lax.axis_size("dp") * lax.axis_size("tensor")
    factor_matrix = adapter_scale / math.sqrt(token_total)
    group_input_rows, group_output_gradient = (
        lax.all_gather(tokens, "tensor", axis=0, tiled=True),
        lax.all_gather(cotangent, "tensor", axis=0, tiled=True),
    )
    input_lowrank = jnp.dot(
        group_input_rows, adapter_first_factors, preferred_element_type=jnp.float32
    ).astype(jnp.bfloat16)
    gate_preactivation = jnp.dot(
        group_input_rows, gate_weight, preferred_element_type=jnp.float32
    ) + adapter_scale * jnp.dot(
        input_lowrank[:, :rank_count], adapter_second_factors[0], preferred_element_type=jnp.float32
    )
    up_preactivation = jnp.dot(
        group_input_rows, up_weight, preferred_element_type=jnp.float32
    ) + adapter_scale * jnp.dot(
        input_lowrank[:, rank_count:], adapter_second_factors[1], preferred_element_type=jnp.float32
    )
    sigmoid = jax.nn.sigmoid(gate_preactivation)
    active = gate_preactivation * sigmoid
    hidden = (active * up_preactivation).astype(jnp.bfloat16)
    hidden_portion = contract_columns(hidden, down_factor_first)
    output_gradient_lowrank = contract_columns(group_output_gradient, down_factor_second).astype(
        jnp.bfloat16
    )
    hidden_gradient = contract_columns(
        group_output_gradient, down_weight
    ) + adapter_scale * jnp.dot(
        output_gradient_lowrank, down_factor_first, preferred_element_type=jnp.float32
    )
    gate_gradient = (
        hidden_gradient * up_preactivation * sigmoid * (1.0 + gate_preactivation * (1.0 - sigmoid))
    ).astype(jnp.bfloat16)
    up_gradient = (hidden_gradient * active).astype(jnp.bfloat16)
    adapter_second_gradient = factor_matrix * jnp.stack(
        [
            contraction_rows(input_lowrank[:, :rank_count], gate_gradient),
            contraction_rows(input_lowrank[:, rank_count:], up_gradient),
        ]
    )
    down_first_gradient = factor_matrix * contraction_rows(output_gradient_lowrank, hidden)
    adapter_second_gradient, down_first_gradient = lax.psum(
        (adapter_second_gradient, down_first_gradient), "dp"
    )
    low_part = jnp.concatenate(
        [
            contract_columns(gate_gradient, adapter_second_factors[0]),
            contract_columns(up_gradient, adapter_second_factors[1]),
            hidden_portion,
        ],
        axis=1,
    )
    term = contract_columns(gate_gradient, gate_weight) + contract_columns(up_gradient, up_weight)
    rounded = lax.optimization_barrier(term.astype(jnp.bfloat16))
    frozen_matrix = lax.psum_scatter(
        rounded.astype(jnp.float32).astype(jnp.bfloat16), "tensor", scatter_dimension=0, tiled=True
    ).astype(jnp.float32)
    group_low = lax.psum(low_part, "tensor")
    lowrank_group = group_low[:, : 2 * rank_count]
    hid_low = group_low[:, 2 * rank_count :]
    adapter_first_gradient = factor_matrix * exact_rows(group_input_rows, lowrank_group)
    down_second_gradient = factor_matrix * exact_rows(hid_low, group_output_gradient)
    adapter_first_gradient, down_second_gradient = lax.psum(
        (adapter_first_gradient, down_second_gradient), "dp"
    )
    lowrank_local = lax.dynamic_slice_in_dim(
        lowrank_group, lax.axis_index("tensor") * tok_rows, tok_rows, 0
    )
    input_gradient = (
        frozen_matrix + adapter_scale * exact_columns(lowrank_local, adapter_first_factors)
    ).astype(jnp.bfloat16)
    return (
        input_gradient,
        adapter_first_gradient,
        adapter_second_gradient,
        down_first_gradient,
        down_second_gradient,
    )


def solution(mesh):
    in_specs = (
        P(("dp", "tensor"), None),
        P(("dp", "tensor"), None),
        P(None, "tensor"),
        P(None, "tensor"),
        P("tensor", None),
        P(),
        P(None, None, "tensor"),
        P(None, "tensor"),
        P(),
    )
    out_specs = (P(("dp", "tensor"), None), P(), P(None, None, "tensor"), P(None, "tensor"), P())
    return jax.shard_map(shards, mesh=mesh, in_specs=in_specs, out_specs=out_specs, check_vma=False)
```

profile of v0, /device:TPU:0, one launch (start us, length us, event | category | flops | bytes accessed | tf_op | source)
XLA Modules:
  0.0 342.5 jit_solution(10707778910616094669)
XLA Ops:
  7.2 0.0 copy-start
  7.2 0.0 all-gather.5.cloned.1.call-start
  7.2 0.7 all-gather.5.cloned.1.call-update
  7.9 0.0 all-gather.3.cloned.1.call-start
  8.0 0.7 all-gather.3.cloned.1.call-update
  8.7 0.0 all-reduce.4.cloned.1.call-start
  8.7 46.3 %all-gather.5.cloned.1.call-done = bf16[512,3584]{1,0:T(8,128)(2,1)} async-done(((bf16[64,3584]{1,0:T(8,128)(2,1)}), bf16[512,3584]{1,0:T(8,128)(2,1)}) %all-gather.5.cloned.1.call-update) | async-done | bytes 3670032 | tf_op jit(solution)/shard_map/all_gather | solution.py:59
  55.0 3.5 %convolution_convert_fusion = bf16[512,128]{0,1:T(8,128)(2,1)S(1)} fusion(bf16[512,3584]{1,0:T(8,128)(2,1)} %all-gather.5.cloned.1.call-done, bf16[3584,128]{1,0:T(8,128)(2,1)S(1)} %copy-done), kind=kOutput, calls=%fused_computation.21 | convolution fusion | flops 469827584 | bytes 4718592 | tf_op jit(solution)/shard_map/dot_general | solution.py:62
  58.5 0.0 copy-start.6
  58.5 0.0 copy-start.10
  58.6 7.5 %fusion.27 = f32[512,1280]{1,0:T(8,128)S(1)} fusion(bf16[512,3584]{1,0:T(8,128)(2,1)S(1)} %copy-done.1, bf16[3584,1280]{1,0:T(8,128)(2,1)} %param.11), kind=kOutput, calls=%fused_computation.45 | convolution fusion | flops 4697620480 | bytes 15466496 | tf_op jit(solution)/shard_map/dot_general | solution.py:65
  66.1 0.0 copy-start.14
  66.1 2.1 fusion.3
  68.2 30.0 %all-gather.3.cloned.1.call-done = bf16[512,3584]{1,0:T(8,128)(2,1)} async-done(((bf16[64,3584]{1,0:T(8,128)(2,1)}), bf16[512,3584]{1,0:T(8,128)(2,1)}) %all-gather.3.cloned.1.call-update) | async-done | bytes 3670032 | tf_op jit(solution)/shard_map/all_gather | solution.py:60
  98.1 3.4 convolution_convert_fusion.1
  101.6 0.0 copy-start.12
  101.6 0.0 slice-start.2
  101.6 0.0 slice-start.3
  101.6 7.7 %fusion.25 = f32[512,1280]{1,0:T(8,128)S(1)} fusion(bf16[512,3584]{1,0:T(8,128)(2,1)S(1)} %copy-done.3, bf16[1280,3584]{1,0:T(8,128)(2,1)} %param.13), kind=kOutput, calls=%fused_computation.43 | convolution fusion | flops 4697620480 | bytes 15466496 | tf_op jit(solution)/shard_map/dot_general | solution.py:18
  109.3 0.5 fusion.5
  109.8 1.5 copy-done.2
  111.3 4.9 %fusion.26 = f32[512,1280]{1,0:T(8,128)S(1)} fusion(bf16[512,3584]{1,0:T(8,128)(2,1)S(1)} %copy-done.2, bf16[3584,1280]{1,0:T(8,128)(2,1)S(1)} %bitcast.46), kind=kOutput, calls=%fused_computation.44 | convolution fusion | flops 4697620480 | bytes 15466496 | tf_op jit(solution)/shard_map/dot_general | solution.py:70
  116.2 1.9 multiply_convert_fusion
  118.1 1.1 convolution_bitcast_fusion
  119.2 0.5 fusion.10
  119.7 1.1 convolution_bitcast_fusion.1
  120.8 0.5 fusion.7
  121.3 0.5 fusion.29
  121.8 1.1 convolution_multiply_fusion.6
  122.9 0.8 pad_maximum_fusion
  123.7 0.0 all-reduce.4.cloned.1.call-update
  123.7 0.2 all-reduce.6.cloned.1.call-start
  124.0 2.0 maximum_multiply_fusion
  125.9 52.4 %all-reduce.4.cloned.1.call-done = f32[512,192]{0,1:T(8,128)} async-done(((f32[512,192]{0,1:T(8,128)}), f32[512,192]{0,1:T(8,128)}) %all-reduce.4.cloned.1.call-update) | async-done | bytes 393232 | tf_op jit(solution)/shard_map/psum | solution.py:114
  178.3 5.1 %fusion = f32[3584,128]{0,1:T(8,128)} fusion(bf16[512,3584]{1,0:T(8,128)(2,1)} %all-gather.5.cloned.1.call-done, f32[512,192]{0,1:T(8,128)} %all-reduce.4.cloned.1.call-done), kind=kOutput, calls=%fused_computation.2 | convolution fusion | flops 2819031040 | bytes 5767168 | tf_op jit(solution)/shard_map/dot_general | solution.py:24
  183.4 3.0 convolution_multiply_fusion.2
  186.4 0.0 all-reduce.6.cloned.1.call-update
  186.4 0.0 reduce-scatter.2.cloned.1.call-start
  186.5 10.6 %fusion.28 = f32[512,3584]{1,0:T(8,128)} fusion(bf16[512,1280]{1,0:T(8,128)(2,1)S(1)} %get-tuple-element.15, bf16[3584,1280]{1,0:T(8,128)(2,1)} %param.11), kind=kOutput, calls=%fused_computation.46 | convolution fusion | flops 4697620480 | bytes 17825792 | tf_op jit(solution)/shard_map/dot_general | solution.py:18
  197.1 11.3 %add_convert_fusion = bf16[512,3584]{1,0:T(8,128)(2,1)} fusion(f32[512,3584]{1,0:T(8,128)} %fusion.28, bf16[512,1280]{1,0:T(8,128)(2,1)S(1)} %get-tuple-element.16, bf16[3584,1280]{1,0:T(8,128)(2,1)} %param.12), kind=kOutput, calls=%fused_computation | convolution fusion | flops 4701290496 | bytes 21495808 | tf_op jit(solution)/shard_map/dot_general | solution.py:18
  208.3 0.0 reduce-scatter.2.cloned.1.call-update
  208.4 74.8 %all-reduce.6.cloned.1.call-done = (f32[3584,128]{0,1:T(8,128)}, f32[2,64,1280]{2,1,0:T(8,128)}, f32[64,1280]{1,0:T(8,128)}, f32[64,3584]{1,0:T(8,128)}) async-done(((f32[3584,128]{0,1:T(8,128)}, f32[2,64,1280]{2,1,0:T(8,128)}, f32[64,1280]{1,0:T(8,128)}, f32[64,3584]{1,0:T(8,128)}), (f32[3584,128]{0,1:T(8,128)}, f32[2,64,1280]{2,1,0:T(8,128)}, f32[64,1280]{1,0:T(8,128)}, ...) | async-done | bytes 3735568 | tf_op jit(solution)/shard_map/psum | solution.py:119
  283.2 2.8 copy.14
  286.0 44.5 %reduce-scatter.2.cloned.1.call-done = bf16[64,3584]{1,0:T(8,128)(2,1)} async-done(((bf16[512,3584]{1,0:T(8,128)(2,1)}), bf16[64,3584]{1,0:T(8,128)(2,1)}) %reduce-scatter.2.cloned.1.call-update) | async-done | bytes 458768 | tf_op jit(solution)/shard_map/reduce_scatter | solution.py:111
  330.6 3.0 fusion.2
  333.5 0.8 copy.20
  334.4 0.7 copy.21
  335.1 0.9 copy.22
  (33 shorter events, 0.1 us)
Async XLA Ops:
  7.2 47.8 %copy-start = (bf16[3584,128]{1,0:T(8,128)(2,1)S(1)}, bf16[3584,128]{1,0:T(8,128)(2,1)}, u32[]{:S(2)}) copy-start(bf16[3584,128]{1,0:T(8,128)(2,1)} %param.14) | copy-start | bytes 2752516
  7.2 47.8 %all-gather.5.cloned.1.call-start = ((), (), s32[]{:S(2)}) async-start(), calls=%async_computation.2 | async-start | bytes 4128768 | tf_op jit(solution)/shard_map/all_gather | solution.py:59
  7.9 90.2 %all-gather.3.cloned.1.call-start = ((), (), s32[]{:S(2)}) async-start(), calls=%async_computation.1 | async-start | bytes 4128768 | tf_op jit(solution)/shard_map/all_gather | solution.py:60
  8.7 169.7 %all-reduce.4.cloned.1.call-start = ((), (), s32[]{:S(2)}) async-start(), calls=%async_computation.4 | async-start | bytes 786432 | tf_op jit(solution)/shard_map/psum | solution.py:114
  55.0 3.5 %copy-start.1 = (bf16[512,3584]{1,0:T(8,128)(2,1)S(1)}, bf16[512,3584]{1,0:T(8,128)(2,1)}, u32[]{:S(2)}) copy-start(bf16[512,3584]{1,0:T(8,128)(2,1)} %all-gather.5.cloned.1.call-done) | copy-start | bytes 11010052
  58.5 7.5 %copy-start.6 = (bf16[512,128]{0,1:T(8,128)(2,1)}, bf16[512,128]{0,1:T(8,128)(2,1)S(1)}, u32[]{:S(2)}) copy-start(bf16[512,128]{0,1:T(8,128)(2,1)S(1)} %convolution_convert_fusion) | copy-start | bytes 393220
  58.5 7.5 %copy-start.10 = (bf16[2,64,1280]{2,1,0:T(8,128)(2,1)S(1)}, bf16[2,64,1280]{2,1,0:T(8,128)(2,1)}, u32[]{:S(2)}) copy-start(bf16[2,64,1280]{2,1,0:T(8,128)(2,1)} %param.15) | copy-start | bytes 983044
  66.1 32.1 %copy-start.14 = (bf16[64,3584]{1,0:T(8,128)(2,1)S(1)}, bf16[64,3584]{1,0:T(8,128)(2,1)}, u32[]{:S(2)}) copy-start(bf16[64,3584]{1,0:T(8,128)(2,1)} %param.17) | copy-start | bytes 1376260
  98.1 3.4 copy-start.3
  98.1 11.7 %slice-start.1 = ((s8[9175040]{0:T(1024)(128)(4,1)}), s8[4194304]{0:T(1024)(128)(4,1)S(1)}, s32[]{:S(2)}) async-start(s8[9175040]{0:T(1024)(128)(4,1)} %bitcast.45), calls=%async_computation.7 | async-start | bytes 8388608
  101.6 7.7 %copy-start.12 = (bf16[64,1280]{1,0:T(8,128)(2,1)S(1)}, bf16[64,1280]{1,0:T(8,128)(2,1)}, u32[]{:S(2)}) copy-start(bf16[64,1280]{1,0:T(8,128)(2,1)} %param.16) | copy-start | bytes 491524
  101.6 8.2 %slice-start.2 = ((s8[9175040]{0:T(1024)(128)(4,1)}), s8[4194304]{0:T(1024)(128)(4,1)S(1)}, s32[]{:S(2)}) async-start(s8[9175040]{0:T(1024)(128)(4,1)} %bitcast.45), calls=%async_computation.8 | async-start | bytes 8388608
  101.6 8.2 %slice-start.3 = ((s8[9175040]{0:T(1024)(128)(4,1)}), s8[786432]{0:T(1024)(128)(4,1)S(1)}, s32[]{:S(2)}) async-start(s8[9175040]{0:T(1024)(128)(4,1)} %bitcast.45), calls=%async_computation.9 | async-start | bytes 1572864
  109.3 2.0 copy-start.2
  111.3 4.9 %copy-start.5 = (f32[512,1280]{1,0:T(8,128)S(1)}, f32[512,1280]{1,0:T(8,128)}, u32[]{:S(2)}) copy-start(f32[512,1280]{1,0:T(8,128)} %fusion.3) | copy-start | bytes 7864324
  111.3 4.9 %copy-start.7 = (bf16[512,128]{0,1:T(8,128)(2,1)S(1)}, bf16[512,128]{0,1:T(8,128)(2,1)}, u32[]{:S(2)}) copy-start(bf16[512,128]{0,1:T(8,128)(2,1)} %copy-done.6) | copy-start | bytes 393220
  111.3 4.9 %copy-start.11 = (bf16[2,64,1280]{2,1,0:T(8,128)(2,1)S(1)}, bf16[2,64,1280]{2,1,0:T(8,128)(2,1)}, u32[]{:S(2)}) copy-start(bf16[2,64,1280]{2,1,0:T(8,128)(2,1)} %param.15) | copy-start | bytes 983044
  123.7 159.5 %all-reduce.6.cloned.1.call-start = ((), (), s32[]{:S(2)}) async-start(), calls=%async_computation.5 | async-start | bytes 7471104 | tf_op jit(solution)/shard_map/psum | solution.py:119
  178.3 5.1 %copy-start.4 = (bf16[512,3584]{1,0:T(8,128)(2,1)S(1)}, bf16[512,3584]{1,0:T(8,128)(2,1)}, u32[]{:S(2)}) copy-start(bf16[512,3584]{1,0:T(8,128)(2,1)} %all-gather.3.cloned.1.call-done) | copy-start | bytes 11010052
  178.3 5.1 %copy-start.8 = (f32[512,192]{0,1:T(8,128)S(1)}, f32[512,192]{0,1:T(8,128)}, u32[]{:S(2)}) copy-start(f32[512,192]{0,1:T(8,128)} %all-reduce.4.cloned.1.call-done) | copy-start | bytes 1179652
  186.4 144.1 %reduce-scatter.2.cloned.1.call-start = ((), (), s32[]{:S(2)}) async-start(), calls=%async_computation.3 | async-start | bytes 4128768 | tf_op jit(solution)/shard_map/reduce_scatter | solution.py:111
  208.4 122.2 %slice-start = ((f32[512,192]{0,1:T(8,128)}), f32[512,128]{0,1:T(8,128)S(1)}, s32[]{:S(2)}) async-start(f32[512,192]{0,1:T(8,128)} %all-reduce.4.cloned.1.call-done), calls=%async_computation.6 | async-start | bytes 524288 | tf_op jit(solution)/shard_map/slice | solution.py:115
  283.2 50.3 %copy-start.13 = (f32[2,64,1280]{2,1,0:T(8,128)S(1)}, f32[2,64,1280]{2,1,0:T(8,128)}, u32[]{:S(2)}) copy-start(f32[2,64,1280]{2,1,0:T(8,128)} %get-tuple-element.19) | copy-start | bytes 1966084
  283.2 51.2 %copy-start.15 = (f32[64,1280]{1,0:T(8,128)S(1)}, f32[64,1280]{1,0:T(8,128)}, u32[]{:S(2)}) copy-start(f32[64,1280]{1,0:T(8,128)} %get-tuple-element.20) | copy-start | bytes 983044
  286.0 49.1 %copy-start.9 = (f32[64,3584]{1,0:T(8,128)S(1)}, f32[64,3584]{1,0:T(8,128)}, u32[]{:S(2)}) copy-start(f32[64,3584]{1,0:T(8,128)} %get-tuple-element.21) | copy-start | bytes 2752516
Sparse Core Ops, SparseCore 0:
  9.7 45.2 all-gather.4
  56.6 41.4 all-gather.2
  123.9 54.4 all-reduce.3
  186.5 96.6 all-reduce.5
  285.5 45.0 reduce-scatter.1
where the time goes:
time: 343 us
  waiting for transfers between devices  249 us (73%)
  matrix products  69.1 us (20%)
  between operations  14 us (4%)
  local copies, waits for them, and re-layouts  6.85 us (2%)
    psum x1, waiting for transfers between devices, shards(): lax.psum((adapter_first_gradient, down_second_gradient), 'dp')  74.8 us
    psum x1, waiting for transfers between devices, shards(): group_low = lax.psum(low_part, 'tensor')  52.4 us
    all_gather x1, waiting for transfers between devices, shards(): lax.all_gather(tokens, 'tensor', axis=0, tiled=True)  46.3 us
    reduce_scatter x1, waiting for transfers between devices, shards(): lax.psum_scatter(rounded.astype(jnp.float32).astype(jnp.bfloat16), 'tenso...  44.5 us
    dot_general x7, matrix products, contract_columns(): lax.dot_general(left, right, (((1,), (1,)), ((), ())), preferred_element_...  34.4 us
    all_gather x1, waiting for transfers between devices, shards(): lax.all_gather(cotangent, 'tensor', axis=0, tiled=True)  30 us
    dot_general x2, matrix products, exact_rows(): lax.dot_general(left.astype(jnp.float32), right.astype(jnp.float32), (((0...  8.06 us
    dot_general x1, matrix products, shards(): jnp.dot(group_input_rows, gate_weight, preferred_element_type=jnp.float32)  7.49 us
  transfers between devices with their start and end apart: 5, of which 5 were waited for; matrix products, arithmetic and copies ran while one was open for 12% of the time, Pallas kernels for 0%

commit v1 on v0

v1 whole, which is shorter than its diff:
```python
import functools
import math

import jax
import jax.numpy as jnp
from jax import lax
from jax.experimental import pallas as pl
from jax.experimental.pallas import tpu as pltpu
from jax.sharding import PartitionSpec as P

adapter_scale = 0.5
bf16 = jnp.bfloat16
f32 = jnp.float32
MESH = pl.DeviceIdType.MESH


def dot(a, b):
    return jnp.dot(a, b, preferred_element_type=f32)


def dot_nt(a, b):
    return lax.dot_general(a, b, (((1,), (1,)), ((), ())), preferred_element_type=f32)


def kernel(
    n, m, T, H, R, TW, W, CW,
    x_ref, dy_ref, wg_ref, wu_ref, wd_ref, a1_ref, a2_ref, df_ref, d2_ref,
    ig_ref, g_ref, p_ref,
    xg, dyg, wg, wu, wd, gate, up, dgate, dup, hid,
    xlow, xlow_t, dylow, dylow_t, low, lowb, lowr, ulow, u_own,
    pb, precv, term, die, rsr, piece, piecer, gbuf,
    load_sem, x_s, x_r, dy_s, dy_r, low_s, low_r, ul_s, ul_r,
    p_s, p_r, die_s, die_r, rs_s, rs_r, pc_s, pc_r, g_s, g_r,
):
    t = lax.axis_index("tensor")
    d = lax.axis_index("dp")
    nz = n // 2
    core = lax.rem(t, 2)
    z = lax.div(t, 2)
    G = n * T
    D = x_ref.shape[1]
    NC = D // W
    NT = H // TW
    nch = D // CW

    def rows(b):
        return pl.ds(pl.multiple_of(b * T, T), T)

    loads = [
        pltpu.make_async_copy(src, dst, load_sem.at[i])
        for i, (src, dst) in enumerate(
            [(x_ref, xg.at[rows(t)]), (dy_ref, dyg.at[rows(t)]), (wg_ref, wg), (wu_ref, wu), (wd_ref, wd)]
        )
    ]
    for c in loads:
        c.start()

    barrier = pltpu.get_barrier_semaphore()
    for k in range(1, n):
        pl.semaphore_signal(barrier, inc=1, device_id={"tensor": lax.rem(t + k, n)}, device_id_type=MESH)
    for k in range(1, m):
        pl.semaphore_signal(barrier, inc=1, device_id={"dp": lax.rem(d + k, m)}, device_id_type=MESH)
    pl.semaphore_wait(barrier, n - 1 + m - 1)

    right = lax.rem(t + 1, n)
    left = lax.rem(t + n - 1, n)

    def hop(at, s_sem, r_sem, side, b):
        return pltpu.make_async_remote_copy(
            src_ref=at(b), dst_ref=at(b), send_sem=s_sem.at[side, b], recv_sem=r_sem.at[b],
            device_id={"tensor": right if side == 0 else left}, device_id_type=MESH,
        )

    def forward(at, s_sem, r_sem, s, limit, first):
        b = t - s

        @pl.when(jnp.logical_and(b >= 0, b < limit))
        def _():
            if not first:
                hop(at, s_sem, r_sem, 0, b).wait_recv()

            @pl.when(t < n - 1)
            def _():
                hop(at, s_sem, r_sem, 0, b).start()

        b2 = t + s

        @pl.when(b2 < limit)
        def _():
            if not first:
                hop(at, s_sem, r_sem, 1, b2).wait_recv()

            @pl.when(t > 0)
            def _():
                hop(at, s_sem, r_sem, 1, b2).start()

    def drain(at, s_sem, r_sem, limit):
        def body(b, carry):
            @pl.when(jnp.logical_and(b <= t, t < n - 1))
            def _():
                hop(at, s_sem, r_sem, 0, b).wait_send()

            @pl.when(jnp.logical_and(b >= t, t > 0))
            def _():
                hop(at, s_sem, r_sem, 1, b).wait_send()

            return carry

        lax.fori_loop(0, limit, body, 0)

    def x_at(b):
        return xg.at[rows(b)]

    def dy_at(b):
        return dyg.at[rows(b)]

    def g_at(b):
        return gbuf.at[b]

    def loop(lo, hi, body):
        def step(i, carry):
            body(i)
            return carry

        lax.fori_loop(lo, hi, step, 0)

    loads[0].wait()
    loads[1].wait()
    forward(x_at, x_s, x_r, 0, n, True)
    loop(1, n, lambda s: forward(x_at, x_s, x_r, s, n, False))

    forward(dy_at, dy_s, dy_r, 0, n, True)
    xl = dot(xg[...], a1_ref[...])
    xlow[...] = xl.astype(bf16)
    xlow_t[...] = xl.T.astype(bf16)
    loads[2].wait()
    loads[3].wait()

    def forward_tile(j):
        cols = pl.ds(pl.multiple_of(j * TW, TW), TW)
        gate[:, cols] = dot(xg[...], wg[:, cols]) + adapter_scale * dot(xlow[:, :R], a2_ref[0, :, cols])
        up[:, cols] = dot(xg[...], wu[:, cols]) + adapter_scale * dot(xlow[:, R:], a2_ref[1, :, cols])

    def dy_step(s):
        forward(dy_at, dy_s, dy_r, s, n, False)

        @pl.when(s - 1 < NT)
        def _():
            forward_tile(s - 1)

    loop(1, n, dy_step)
    if NT > n - 1:
        loop(n - 1, NT, forward_tile)

    loads[4].wait()
    dl = dot_nt(dyg[...], d2_ref[...])
    dylow[...] = dl.astype(bf16)
    dylow_t[...] = dl.T.astype(bf16)
    low[...] = jnp.zeros_like(low)

    def backward_tile(j):
        cols = pl.ds(pl.multiple_of(j * TW, TW), TW)
        dh = dot_nt(dyg[...], wd[cols, :]) + adapter_scale * dot(dylow[...], df_ref[:, cols])
        gp = gate[:, cols]
        u = up[:, cols]
        sig = jax.nn.sigmoid(gp)
        act = gp * sig
        dg = (dh * u * sig * (1.0 + gp * (1.0 - sig))).astype(bf16)
        du = (dh * act).astype(bf16)
        hd = (act * u).astype(bf16)
        dgate[:, cols] = dg
        dup[:, cols] = du
        pb[:R, cols] = dot(xlow_t[:R, :], dg).astype(bf16)
        pb[R : 2 * R, cols] = dot(xlow_t[R:, :], du).astype(bf16)
        pb[2 * R :, cols] = dot(dylow_t[...], hd).astype(bf16)
        low[:, :R] += dot_nt(dg, a2_ref[0, :, cols])
        low[:, R : 2 * R] += dot_nt(du, a2_ref[1, :, cols])
        low[:, 2 * R :] += dot_nt(hd, df_ref[:, cols])

    loop(0, NT, backward_tile)

    lowb[...] = low[...].astype(bf16)

    def low_copy(k):
        peer = lax.rem(t + k, n)
        return pltpu.make_async_remote_copy(
            src_ref=lowb.at[rows(peer)], dst_ref=lowr.at[t], send_sem=low_s.at[k], recv_sem=low_r.at[t],
            device_id={"tensor": peer}, device_id_type=MESH,
        )

    def low_arrival(k):
        peer = lax.rem(t + k, n)
        return pltpu.make_async_remote_copy(
            src_ref=lowb.at[rows(peer)], dst_ref=lowr.at[peer], send_sem=low_s.at[k], recv_sem=low_r.at[peer],
            device_id={"tensor": peer}, device_id_type=MESH,
        )

    def ul_copy(k, b):
        peer = lax.rem(t + k, n)
        return pltpu.make_async_remote_copy(
            src_ref=ulow.at[rows(b)], dst_ref=ulow.at[rows(b)], send_sem=ul_s.at[k], recv_sem=ul_r.at[b],
            device_id={"tensor": peer}, device_id_type=MESH,
        )

    def dp_copy(src, dst, s_sem, r_sem, k, slot):
        peer = lax.rem(d + k, m)
        return pltpu.make_async_remote_copy(
            src_ref=src, dst_ref=dst.at[slot], send_sem=s_sem.at[k], recv_sem=r_sem.at[slot],
            device_id={"dp": peer}, device_id_type=MESH,
        )

    loop(1, n, lambda k: low_copy(k).start())
    loop(1, m, lambda k: dp_copy(pb, precv, p_s, p_r, k, d).start())

    partner = t + 1 - 2 * core

    def die_copy(c):
        return pltpu.make_async_remote_copy(
            src_ref=term.at[c, 1 - core], dst_ref=die.at[c], send_sem=die_s.at[c], recv_sem=die_r.at[c],
            device_id={"tensor": partner}, device_id_type=MESH,
        )

    def rs_copy(c, k, slot):
        other = lax.rem(z + k, nz)
        return pltpu.make_async_remote_copy(
            src_ref=term.at[c, core, other], dst_ref=rsr.at[c, slot], send_sem=rs_s.at[c, k],
            recv_sem=rs_r.at[c, slot], device_id={"tensor": 2 * other + core}, device_id_type=MESH,
        )

    def chip_sum(c):
        die_copy(c).wait_recv()
        term[c, core] = (term[c, core].astype(f32) + die[c].astype(f32)).astype(bf16)
        for k in range(1, nz):
            rs_copy(c, k, z).start()

    def term_tile(c):
        span = pl.ds(pl.multiple_of(c * W, W), W)
        v = (dot_nt(dgate[...], wg[span, :]) + dot_nt(dup[...], wu[span, :])).astype(bf16)
        v = v.reshape(nz, 2, T, W)
        term[c, 0] = v[:, 0]
        term[c, 1] = v[:, 1]
        die_copy(c).start()

        @pl.when(c > 0)
        def _():
            chip_sum(c - 1)

    cut1, cut2, cut3 = NC // 4, NC // 2, (3 * NC) // 4
    loop(0, cut1, term_tile)

    lowr[t] = lowb[rows(t), :]
    loop(1, n, lambda k: low_arrival(k).wait_recv())
    total = lowr[0].astype(f32)
    for b in range(1, n):
        total = total + lowr[b].astype(f32)
    u_own[...] = total.astype(bf16)
    ulow[rows(t), :] = total.astype(bf16)
    loop(1, n, lambda k: ul_copy(k, t).start())

    loop(cut1, cut2, term_tile)

    loop(1, n, lambda k: ul_copy(k, lax.rem(t + k, n)).wait_recv())

    @pl.when(t < nch)
    def _():
        cols = pl.ds(pl.multiple_of(t * CW, CW), CW)
        u_t = ulow[...].astype(f32).T.astype(bf16)
        piece[: 2 * R, :] = dot(u_t[: 2 * R], xg[:, cols]).astype(bf16)
        piece[2 * R :, :] = dot(u_t[2 * R :], dyg[:, cols]).astype(bf16)
        loop(1, m, lambda k: dp_copy(piece, piecer, pc_s, pc_r, k, d).start())

    loop(cut2, cut3, term_tile)

    @pl.when(t < nch)
    def _():
        piecer[d] = piece[...]
        loop(1, m, lambda k: dp_copy(piece, piecer, pc_s, pc_r, k, lax.rem(d + k, m)).wait_recv())
        acc = piecer[0].astype(f32)
        for e in range(1, m):
            acc = acc + piecer[e].astype(f32)
        gbuf[t] = acc.astype(bf16)
        forward(g_at, g_s, g_r, 0, nch, True)

    loop(cut3, NC, term_tile)
    chip_sum(NC - 1)

    precv[d] = pb[...]
    loop(1, m, lambda k: dp_copy(pb, precv, p_s, p_r, k, lax.rem(d + k, m)).wait_recv())
    acc = precv[0].astype(f32)
    for e in range(1, m):
        acc = acc + precv[e].astype(f32)
    p_ref[...] = acc

    loop(1, n, lambda s: forward(g_at, g_s, g_r, s, nch, False))
    g_ref[...] = gbuf[...]

    def finish(c):
        span = pl.ds(pl.multiple_of(c * W, W), W)
        total = term[c, core, z].astype(f32) + adapter_scale * dot_nt(u_own[:, : 2 * R], a1_ref[span, :])
        for k in range(1, nz):
            other = lax.rem(z + k, nz)
            rs_copy(c, k, other).wait_recv()
            total = total + rsr[c, other].astype(f32)
        ig_ref[:, span] = total.astype(bf16)

    loop(0, NC, finish)

    drain(x_at, x_s, x_r, n)
    drain(dy_at, dy_s, dy_r, n)
    drain(g_at, g_s, g_r, nch)
    loop(1, n, lambda k: low_copy(k).wait_send())
    loop(1, n, lambda k: ul_copy(k, t).wait_send())
    loop(1, m, lambda k: dp_copy(pb, precv, p_s, p_r, k, d).wait_send())

    @pl.when(t < nch)
    def _():
        loop(1, m, lambda k: dp_copy(piece, piecer, pc_s, pc_r, k, d).wait_send())

    def sent(c):
        die_copy(c).wait_send()
        for k in range(1, nz):
            rs_copy(c, k, z).wait_send()

    loop(0, NC, sent)


def shards(x, dy, wg, wu, wd, a1, a2, df, d2):
    n = lax.axis_size("tensor")
    m = lax.axis_size("dp")
    T, D = x.shape
    H = wg.shape[1]
    R = a2.shape[1]
    G = n * T
    TW = 256 if H % 256 == 0 else 128
    W = 256
    NC = D // W
    CW = -(-D // (n * 128)) * 128
    nch = D // CW
    factor = adapter_scale / math.sqrt(T * n * m)
    nz = n // 2
    V = pltpu.VMEM
    DMA = pltpu.SemaphoreType.DMA
    any_spec = pl.BlockSpec(memory_space=pl.ANY)
    vmem_spec = pl.BlockSpec(memory_space=pltpu.VMEM)
    macs = 5 * G * D * H
    ig, g, p = pl.pallas_call(
        functools.partial(kernel, n, m, T, H, R, TW, W, CW),
        out_shape=(
            jax.ShapeDtypeStruct((T, D), bf16),
            jax.ShapeDtypeStruct((nch, 3 * R, CW), bf16),
            jax.ShapeDtypeStruct((3 * R, H), f32),
        ),
        in_specs=[any_spec] * 5 + [vmem_spec] * 4,
        out_specs=(vmem_spec,) * 3,
        scratch_shapes=[
            V((G, D), bf16), V((G, D), bf16),
            V((D, H), bf16), V((D, H), bf16), V((H, D), bf16),
            V((G, H), f32), V((G, H), f32),
            V((G, H), bf16), V((G, H), bf16), V((8, 128), bf16),
            V((G, 2 * R), bf16), V((2 * R, G), bf16), V((G, R), bf16), V((R, G), bf16),
            V((G, 3 * R), f32), V((G, 3 * R), bf16), V((n, T, 3 * R), bf16),
            V((G, 3 * R), bf16), V((T, 3 * R), bf16),
            V((3 * R, H), bf16), V((m, 3 * R, H), bf16),
            V((NC, 2, nz, T, W), bf16), V((NC, nz, T, W), bf16), V((NC, nz, T, W), bf16),
            V((3 * R, CW), bf16), V((m, 3 * R, CW), bf16), V((nch, 3 * R, CW), bf16),
            DMA((5,)),
            DMA((2, n)), DMA((n,)), DMA((2, n)), DMA((n,)),
            DMA((n,)), DMA((n,)), DMA((n,)), DMA((n,)),
            DMA((m,)), DMA((m,)),
            DMA((NC,)), DMA((NC,)), DMA((NC, nz)), DMA((NC, nz)),
            DMA((m,)), DMA((m,)), DMA((2, n)), DMA((n,)),
        ],
        compiler_params=pltpu.CompilerParams(
            collective_id=0, has_side_effects=True, vmem_limit_bytes=63 * 1024 * 1024
        ),
        cost_estimate=pl.CostEstimate(flops=2 * macs, bytes_accessed=6 * D * H, transcendentals=G * H),
    )(x, dy, wg, wu, wd, a1, a2, df, d2)
    g = factor * g.astype(f32)
    first = g[:, : 2 * R].transpose(0, 2, 1).reshape(D, 2 * R)
    second = g[:, 2 * R :].transpose(1, 0, 2).reshape(R, D)
    p = factor * p
    return ig, first, p[: 2 * R].reshape(2, R, H), p[2 * R :], second


def solution(mesh):
    in_specs = (
        P(("dp", "tensor"), None),
        P(("dp", "tensor"), None),
        P(None, "tensor"),
        P(None, "tensor"),
        P("tensor", None),
        P(),
        P(None, None, "tensor"),
        P(None, "tensor"),
        P(),
    )
    out_specs = (P(("dp", "tensor"), None), P(), P(None, None, "tensor"), P(None, "tensor"), P())
    return jax.shard_map(shards, mesh=mesh, in_specs=in_specs, out_specs=out_specs, check_vma=False)
```

time: 343 us -> 165 us (0.48)
  waiting for transfers between devices: 249 us -> 0 us
  Pallas kernels: 0 us -> 157 us
  matrix products: 69.1 us -> 0 us
  between operations: 14 us -> 0.69 us
    pallas_call x0 -> x1, Pallas kernels: none -> 157 us  [shards(): pl.pallas_call(functools.partial(kernel, n, m, T, H, R, TW, W, CW), out_s...]
    psum x2 -> x0, waiting for transfers between devices: 127 us -> none  [the longest x1 74.8 us: shards(): lax.psum((adapter_first_gradient, down_second_gradient), 'dp')]
    all_gather x2 -> x0, waiting for transfers between devices: 76.2 us -> none  [the longest x1 46.3 us: shards(): lax.all_gather(tokens, 'tensor', axis=0, tiled=True)]
    dot_general x19 -> x0, matrix products: 69.1 us -> none  [the longest x7 34.4 us: contract_columns(): lax.dot_general(left, right, (((1,), (1,)), ((), ())), preferred_element_...]
    reduce_scatter x1 -> x0, waiting for transfers between devices: 44.5 us -> none  [shards(): lax.psum_scatter(rounded.astype(jnp.float32).astype(jnp.bfloat16), 'tenso...]
    unnamed x42 -> x6, local copies, waits for them, and re-layouts: 6.84 us -> 0.86 us
  transfers between devices with their start and end apart: 5 -> 0, of which waited for: 5 -> 0; matrix products, arithmetic and copies ran while one was open for 12% -> 0% of each run, Pallas kernels for 0% -> 0%
where the time goes in v1:
time: 165 us
  Pallas kernels  157 us (95%)
  local copies, waits for them, and re-layouts  5.31 us (3%)
  other arithmetic  1.8 us (1%)
    pallas_call x1, Pallas kernels, shards(): pl.pallas_call(functools.partial(kernel, n, m, T, H, R, TW, W, CW), out_s...  157 us

profile of v1, /device:TPU:0, one launch (start us, length us, event | category | flops | bytes accessed | tf_op | source)
XLA Modules:
  0.0 165.3 jit_solution(7796129595725535440)
XLA Ops:
  0.6 157.5 %shard_map.128 = (bf16[64,3584]{1,0:T(8,128)(2,1)}, bf16[7,192,512]{2,1,0:T(8,128)(2,1)}, f32[192,1280]{1,0:T(8,128)}) custom-call(bf16[64,3584]{1,0:T(8,128)(2,1)} %x_ref.1, bf16[64,3584]{1,0:T(8,128)(2,1)} %dy_ref.1, bf16[3584,1280]{1,0:T(8,128)(2,1)} %wg_ref.1, bf16[3584,1280]{1,0:T(8,128)(2,1)} %wu_ref.1, bf16[1280,3584]{1,0:T(8,128)(2,1)} %wd_ref.1, ...), custom_call_target="tpu_custom_call" | custom-call | flops 23488102400 | bytes 27525120 | tf_op jit(solution)/shard_map/pallas_call | solution.py:346
  158.1 0.0 copy-start
  158.1 1.4 broadcast_multiply_fusion
  159.5 0.7 slice.18
  160.3 0.9 slice.17
  161.1 0.0 copy-done
  161.1 0.4 convert_multiply_fusion
  161.5 0.1 slice_bitcast_fusion.1
  161.6 0.2 slice_bitcast_fusion
  161.8 0.0 copy-start.1
  161.8 1.7 %copy.14 = f32[7,512,128]{2,1,0:T(8,128)} copy(f32[7,512,128]{1,2,0:T(8,128)S(1)} %slice_bitcast_fusion) | data formatting | bytes 3670016 | tf_op jit(solution)/shard_map/transpose | solution.py:379
  163.5 1.0 copy.16
  164.5 0.0 copy-done.1
  164.5 0.8 copy.18
Async XLA Ops:
  158.1 3.0 %copy-start = (bf16[7,192,512]{2,1,0:T(8,128)(2,1)S(1)}, bf16[7,192,512]{2,1,0:T(8,128)(2,1)}, u32[]{:S(2)}) copy-start(bf16[7,192,512]{2,1,0:T(8,128)(2,1)} %get-tuple-element.9) | copy-start | bytes 4128772
  161.8 2.7 %copy-start.1 = (bf16[64,3584]{1,0:T(8,128)(2,1)S(1)}, bf16[64,3584]{1,0:T(8,128)(2,1)}, u32[]{:S(2)}) copy-start(bf16[64,3584]{1,0:T(8,128)(2,1)} %get-tuple-element.16) | copy-start | bytes 1376260

commit v2 on v1

v2 whole, which is shorter than its diff:
```python
import functools
import math

import jax
import jax.numpy as jnp
from jax import lax
from jax.experimental import pallas as pl
from jax.experimental.pallas import tpu as pltpu
from jax.sharding import PartitionSpec as P

adapter_scale = 0.5
bf16 = jnp.bfloat16
f32 = jnp.float32
MESH = pl.DeviceIdType.MESH


def dot(a, b):
    return jnp.dot(a, b, preferred_element_type=f32)


def dot_nt(a, b):
    return lax.dot_general(a, b, (((1,), (1,)), ((), ())), preferred_element_type=f32)


def kernel(
    n, m, T, H, R, TW, W, cp, cg,
    x_ref, dy_ref, wg_ref, wu_ref, wd_ref, a1_ref, a2_ref, df_ref, d2_ref,
    ig_ref, first_ref, second_ref, p2_ref, p1_ref,
    xg, dyg, wg, wu, wd, gate, up, dgate, dup,
    xlow, xlow_t, dylow, dylow_t, low, lowb, lowr, ulow, u_own,
    pacc, psend, precv, pfin, gsend, grecv, gfin, term, die, rsr,
    load_sem, x_s, x_r, dy_s, dy_r, low_s, low_r, ul_s, ul_r,
    p_s, p_r, pf_s, pf_r, g_s, g_r, gf_s, gf_r, gd_s, gd_r, die_s, die_r, rs_s, rs_r,
):
    t = lax.axis_index("tensor")
    d = lax.axis_index("dp")
    nz = n // 2
    core = lax.rem(t, 2)
    z = lax.div(t, 2)
    partner = t + 1 - 2 * core
    S = T // 2
    D = x_ref.shape[1]
    NC = D // W
    NT = H // TW
    HC = H // 128
    DC = D // 128

    def rows(b):
        return pl.ds(pl.multiple_of(b * S, S), S)

    def loop(lo, hi, body):
        def step(i, carry):
            body(i)
            return carry

        lax.fori_loop(lo, hi, step, 0)

    pairs = []
    for h in range(2):
        part = pl.ds(h * S, S)
        pairs += [(x_ref.at[part], xg.at[h, rows(t)]), (dy_ref.at[part], dyg.at[h, rows(t)])]
    pairs += [(wg_ref, wg), (wu_ref, wu), (wd_ref, wd)]
    loads = [pltpu.make_async_copy(src, dst, load_sem.at[i]) for i, (src, dst) in enumerate(pairs)]
    for c in loads:
        c.start()

    barrier = pltpu.get_barrier_semaphore()
    for k in range(1, n):
        pl.semaphore_signal(barrier, inc=1, device_id={"tensor": lax.rem(t + k, n)}, device_id_type=MESH)
    for k in range(1, m):
        pl.semaphore_signal(barrier, inc=1, device_id={"dp": lax.rem(d + k, m)}, device_id_type=MESH)
    pl.semaphore_wait(barrier, n - 1 + m - 1)

    right = lax.rem(t + 1, n)
    left = lax.rem(t + n - 1, n)

    def hop(line, side, b):
        buf, s_sem, r_sem, h = line
        return pltpu.make_async_remote_copy(
            src_ref=buf.at[h, rows(b)], dst_ref=buf.at[h, rows(b)], send_sem=s_sem.at[h, side, b],
            recv_sem=r_sem.at[h, b], device_id={"tensor": right if side == 0 else left}, device_id_type=MESH,
        )

    def forward(line, s, first=False):
        b = t - s

        @pl.when(b >= 0)
        def _():
            if not first:
                hop(line, 0, b).wait_recv()

            @pl.when(t < n - 1)
            def _():
                hop(line, 0, b).start()

        b2 = t + s

        @pl.when(b2 < n)
        def _():
            if not first:
                hop(line, 1, b2).wait_recv()

            @pl.when(t > 0)
            def _():
                hop(line, 1, b2).start()

    def drain(line):
        def body(b):
            @pl.when(jnp.logical_and(b <= t, t < n - 1))
            def _():
                hop(line, 0, b).wait_send()

            @pl.when(jnp.logical_and(b >= t, t > 0))
            def _():
                hop(line, 1, b).wait_send()

        loop(0, n, body)

    lines_x = [(xg, x_s, x_r, h) for h in range(2)]
    lines_dy = [(dyg, dy_s, dy_r, h) for h in range(2)]

    def tile_cols(j):
        return pl.ds(pl.multiple_of(j * TW, TW), TW)

    def input_rank(h):
        xl = dot(xg[h], a1_ref[...])
        xlow[...] = xl.astype(bf16)
        xlow_t[...] = xl.T.astype(bf16)

    def forward_tile(h, j):
        cols = tile_cols(j)
        gate[:, cols] = dot(xg[h], wg[:, cols]) + adapter_scale * dot(xlow[:, :R], a2_ref[0, :, cols])
        up[:, cols] = dot(xg[h], wu[:, cols]) + adapter_scale * dot(xlow[:, R:], a2_ref[1, :, cols])

    def cotangent_rank(h):
        dl = dot_nt(dyg[h], d2_ref[...])
        dylow[...] = dl.astype(bf16)
        dylow_t[...] = dl.T.astype(bf16)
        low[...] = jnp.zeros_like(low)

    def backward_tile(h, j):
        cols = tile_cols(j)
        dh = dot_nt(dyg[h], wd[cols, :]) + adapter_scale * dot(dylow[...], df_ref[:, cols])
        gp = gate[:, cols]
        u = up[:, cols]
        sig = jax.nn.sigmoid(gp)
        act = gp * sig
        dg = (dh * u * sig * (1.0 + gp * (1.0 - sig))).astype(bf16)
        du = (dh * act).astype(bf16)
        hd = (act * u).astype(bf16)
        dgate[:, cols] = dg
        dup[:, cols] = du
        for i, (a, b) in enumerate([(xlow_t[:R, :], dg), (xlow_t[R:, :], du), (dylow_t[...], hd)]):
            v = dot(a, b)
            if h == 0:
                pacc[i, :, cols] = v
            else:
                pacc[i, :, cols] += v
        low[:, :R] += dot_nt(dg, a2_ref[0, :, cols])
        low[:, R : 2 * R] += dot_nt(du, a2_ref[1, :, cols])
        low[:, 2 * R :] += dot_nt(hd, df_ref[:, cols])

    def keep_low(h):
        lowb[:, h] = low[...].astype(bf16).reshape(n, S, 3 * R)

    def send_to(src, dst, s_sem, r_sem, peer):
        return pltpu.make_async_remote_copy(
            src_ref=src, dst_ref=dst, send_sem=s_sem, recv_sem=r_sem, device_id=peer, device_id_type=MESH
        )

    def low_copy(k, slot):
        peer = lax.rem(t + k, n)
        return send_to(lowb.at[peer], lowr.at[slot], low_s.at[k], low_r.at[slot], {"tensor": peer})

    def ul_copy(k, slot):
        peer = lax.rem(t + k, n)
        return send_to(ulow.at[slot], ulow.at[slot], ul_s.at[k], ul_r.at[slot], {"tensor": peer})

    def scatter_copy(src, dst, s_sem, r_sem, k, slot):
        peer = lax.rem(d + k, m)
        return send_to(src.at[peer], dst.at[slot], s_sem.at[k], r_sem.at[slot], {"dp": peer})

    def p_copy(k, slot):
        return scatter_copy(psend, precv, p_s, p_r, k, slot)

    def g_copy(k, slot):
        return scatter_copy(gsend, grecv, g_s, g_r, k, slot)

    def pf_copy(k, slot):
        peer = lax.rem(d + k, m)
        return send_to(pfin.at[slot], pfin.at[slot], pf_s.at[k], pf_r.at[slot], {"dp": peer})

    def gf_copy(k, slot):
        peer = lax.rem(d + k, m)
        at = gfin.at[core, slot]
        return send_to(at, at, gf_s.at[k], gf_r.at[slot], {"dp": peer})

    def gd_copy(side, slot):
        at = gfin.at[side, slot]
        return send_to(at, at, gd_s.at[slot], gd_r.at[slot], {"tensor": partner})

    def other_d(k):
        return lax.rem(d + k, m)

    def die_copy(h, c):
        return send_to(term.at[h, c, 1 - core], die.at[h, c], die_s.at[h, c], die_r.at[h, c], {"tensor": partner})

    def rs_copy(h, c, k, slot):
        other = lax.rem(z + k, nz)
        return send_to(
            term.at[h, c, core, other], rsr.at[h, c, slot], rs_s.at[h, c, k], rs_r.at[h, c, slot],
            {"tensor": 2 * other + core},
        )

    def chip_sum(h, c):
        die_copy(h, c).wait_recv()
        term[h, c, core] = (term[h, c, core].astype(f32) + die[h, c].astype(f32)).astype(bf16)
        for k in range(1, nz):
            rs_copy(h, c, k, z).start()

    def term_tile(h, c):
        span = pl.ds(pl.multiple_of(c * W, W), W)
        v = (dot_nt(dgate[...], wg[span, :]) + dot_nt(dup[...], wu[span, :])).astype(bf16)
        v = v.reshape(nz, 2, S, W)
        term[h, c, 0] = v[:, 0]
        term[h, c, 1] = v[:, 1]
        die_copy(h, c).start()

        @pl.when(c > 0)
        def _():
            chip_sum(h, c - 1)

    loads[0].wait()
    forward(lines_x[0], 0, True)
    loop(1, n, lambda s: forward(lines_x[0], s))
    loads[1].wait()
    forward(lines_dy[0], 0, True)
    input_rank(0)
    loads[4].wait()
    loads[5].wait()

    def beside(line, s, h, tile):
        forward(line, s)

        @pl.when(s - 1 < NT)
        def _():
            tile(h, s - 1)

    loop(1, n, lambda s: beside(lines_dy[0], s, 0, forward_tile))
    loop(n - 1, NT, lambda j: forward_tile(0, j))

    loads[2].wait()
    forward(lines_x[1], 0, True)
    cotangent_rank(0)
    loads[6].wait()
    loop(1, n, lambda s: beside(lines_x[1], s, 0, backward_tile))
    loop(n - 1, NT, lambda j: backward_tile(0, j))

    loads[3].wait()
    forward(lines_dy[1], 0, True)
    keep_low(0)
    input_rank(1)
    per = -(-NC // (n - 1))

    def mixed(s):
        forward(lines_dy[1], s)
        for i in range(per):
            c = (s - 1) * per + i

            @pl.when(c < NC)
            def _():
                term_tile(0, c)

        @pl.when(s - 1 < NT)
        def _():
            forward_tile(1, s - 1)

    loop(1, n, mixed)
    loop(n - 1, NT, lambda j: forward_tile(1, j))
    chip_sum(0, NC - 1)

    cotangent_rank(1)
    loop(0, NT, lambda j: backward_tile(1, j))
    keep_low(1)

    loop(1, n, lambda k: low_copy(k, t).start())
    for q in range(m * cp):
        g, j = divmod(q, HC)
        if g < 3:
            psend[q // cp, q % cp] = pacc[g, :, 128 * j : 128 * (j + 1)].astype(bf16)
        else:
            psend[q // cp, q % cp] = jnp.zeros((R, 128), bf16)
    loop(1, m, lambda k: p_copy(k, d).start())

    cut1, cut2, cut3 = NC // 4, NC // 2, (3 * NC) // 4
    loop(0, cut1, lambda c: term_tile(1, c))

    lowr[t] = lowb[t]
    loop(1, n, lambda k: low_copy(k, lax.rem(t + k, n)).wait_recv())
    total = lowr[0].astype(f32)
    for b in range(1, n):
        total = total + lowr[b].astype(f32)
    u_own[...] = total.astype(bf16).reshape(T, 3 * R)
    ulow[t] = total.astype(bf16)
    loop(1, n, lambda k: ul_copy(k, t).start())

    loop(cut1, cut2, lambda c: term_tile(1, c))

    loop(1, n, lambda k: ul_copy(k, lax.rem(t + k, n)).wait_recv())
    u_t = [ulow[:, h].reshape(n * S, 3 * R).astype(f32).T.astype(bf16) for h in range(2)]
    for q in range(2 * m * cg):
        g, j = divmod(q, DC)
        if q % (m * cg) == 0:
            owner_side = q // (m * cg)
        if g < 3:
            src = xg if g < 2 else dyg

            @pl.when(core == owner_side)
            def _(q=q, g=g, j=j, src=src):
                acc = 0.0
                for h in range(2):
                    acc = acc + dot(u_t[h][g * R : (g + 1) * R], src[h, :, 128 * j : 128 * (j + 1)])
                gsend[(q // cg) % m, q % cg] = acc.astype(bf16)
        else:

            @pl.when(core == owner_side)
            def _(q=q):
                gsend[(q // cg) % m, q % cg] = jnp.zeros((R, 128), bf16)

    loop(1, m, lambda k: g_copy(k, d).start())

    loop(cut2, cut3, lambda c: term_tile(1, c))

    precv[d] = psend[d]
    loop(1, m, lambda k: p_copy(k, other_d(k)).wait_recv())
    total = precv[0].astype(f32)
    for e in range(1, m):
        total = total + precv[e].astype(f32)
    pfin[d] = total.astype(bf16)
    loop(1, m, lambda k: pf_copy(k, d).start())

    loop(cut3, NC, lambda c: term_tile(1, c))
    chip_sum(1, NC - 1)

    grecv[d] = gsend[d]
    loop(1, m, lambda k: g_copy(k, other_d(k)).wait_recv())
    total = grecv[0].astype(f32)
    for e in range(1, m):
        total = total + grecv[e].astype(f32)
    gfin[core, d] = total.astype(bf16)
    loop(1, m, lambda k: gf_copy(k, d).start())
    gd_copy(core, d).start()

    loop(1, m, lambda k: pf_copy(k, other_d(k)).wait_recv())
    for q in range(3 * HC):
        g, j = divmod(q, HC)
        v = pfin[q // cp, q % cp].astype(f32)
        if g < 2:
            p2_ref[g, :, 128 * j : 128 * (j + 1)] = v
        else:
            p1_ref[:, 128 * j : 128 * (j + 1)] = v

    def finish(h, c):
        span = pl.ds(pl.multiple_of(c * W, W), W)
        part = slice(h * S, (h + 1) * S)
        total = term[h, c, core, z].astype(f32) + adapter_scale * dot_nt(u_own[part, : 2 * R], a1_ref[span, :])
        for k in range(1, nz):
            other = lax.rem(z + k, nz)
            rs_copy(h, c, k, other).wait_recv()
            total = total + rsr[h, c, other].astype(f32)
        ig_ref[part, span] = total.astype(bf16)

    loop(0, NC, lambda c: finish(0, c))

    def pass_on(k):
        gf_copy(k, other_d(k)).wait_recv()
        gd_copy(core, other_d(k)).start()

    loop(1, m, pass_on)
    loop(0, m, lambda e: gd_copy(1 - core, e).wait_recv())

    def g_chunk(g, j):
        q = g * DC + j
        return gfin[q // (m * cg), (q // cg) % m, q % cg].astype(f32)

    for j in range(DC):
        both = jnp.concatenate([g_chunk(0, j), g_chunk(1, j)], axis=0)
        first_ref[128 * j : 128 * (j + 1), :] = both.T
        second_ref[:, 128 * j : 128 * (j + 1)] = g_chunk(2, j)

    loop(0, NC, lambda c: finish(1, c))

    for line in lines_x + lines_dy:
        drain(line)
    loop(1, n, lambda k: low_copy(k, t).wait_send())
    loop(1, n, lambda k: ul_copy(k, t).wait_send())
    loop(1, m, lambda k: p_copy(k, d).wait_send())
    loop(1, m, lambda k: pf_copy(k, d).wait_send())
    loop(1, m, lambda k: g_copy(k, d).wait_send())
    loop(1, m, lambda k: gf_copy(k, d).wait_send())
    loop(0, m, lambda e: gd_copy(core, e).wait_send())

    def sent(c):
        for h in range(2):
            die_copy(h, c).wait_send()
            for k in range(1, nz):
                rs_copy(h, c, k, z).wait_send()

    loop(0, NC, sent)


def shards(x, dy, wg, wu, wd, a1, a2, df, d2):
    n = lax.axis_size("tensor")
    m = lax.axis_size("dp")
    T, D = x.shape
    H = wg.shape[1]
    R = a2.shape[1]
    S = T // 2
    GH = n * S
    TW = 256 if H % 256 == 0 else 128
    W = 256
    NC = D // W
    cp = -(-3 * (H // 128) // m)
    cg = -(-3 * (D // 128) // (2 * m))
    factor = adapter_scale / math.sqrt(T * n * m)
    nz = n // 2
    V = pltpu.VMEM
    DMA = pltpu.SemaphoreType.DMA
    any_spec = pl.BlockSpec(memory_space=pl.ANY)
    vmem_spec = pl.BlockSpec(memory_space=pltpu.VMEM)
    macs = 5 * n * T * D * H
    ig, first, second, p2, p1 = pl.pallas_call(
        functools.partial(kernel, n, m, T, H, R, TW, W, cp, cg),
        out_shape=(
            jax.ShapeDtypeStruct((T, D), bf16),
            jax.ShapeDtypeStruct((D, 2 * R), f32),
            jax.ShapeDtypeStruct((R, D), f32),
            jax.ShapeDtypeStruct((2, R, H), f32),
            jax.ShapeDtypeStruct((R, H), f32),
        ),
        in_specs=[any_spec] * 5 + [vmem_spec] * 4,
        out_specs=(vmem_spec,) * 5,
        scratch_shapes=[
            V((2, GH, D), bf16), V((2, GH, D), bf16),
            V((D, H), bf16), V((D, H), bf16), V((H, D), bf16),
            V((GH, H), f32), V((GH, H), f32), V((GH, H), bf16), V((GH, H), bf16),
            V((GH, 2 * R), bf16), V((2 * R, GH), bf16), V((GH, R), bf16), V((R, GH), bf16),
            V((GH, 3 * R), f32), V((n, 2, S, 3 * R), bf16), V((n, 2, S, 3 * R), bf16),
            V((n, 2, S, 3 * R), bf16), V((T, 3 * R), bf16),
            V((3, R, H), f32), V((m, cp, R, 128), bf16), V((m, cp, R, 128), bf16), V((m, cp, R, 128), bf16),
            V((m, cg, R, 128), bf16), V((m, cg, R, 128), bf16), V((2, m, cg, R, 128), bf16),
            V((2, NC, 2, nz, S, W), bf16), V((2, NC, nz, S, W), bf16), V((2, NC, nz, S, W), bf16),
            DMA((7,)),
            DMA((2, 2, n)), DMA((2, n)), DMA((2, 2, n)), DMA((2, n)),
            DMA((n,)), DMA((n,)), DMA((n,)), DMA((n,)),
            DMA((m,)), DMA((m,)), DMA((m,)), DMA((m,)),
            DMA((m,)), DMA((m,)), DMA((m,)), DMA((m,)), DMA((m,)), DMA((m,)),
            DMA((2, NC)), DMA((2, NC)), DMA((2, NC, nz)), DMA((2, NC, nz)),
        ],
        compiler_params=pltpu.CompilerParams(
            collective_id=0, has_side_effects=True, vmem_limit_bytes=63 * 1024 * 1024
        ),
        cost_estimate=pl.CostEstimate(flops=2 * macs, bytes_accessed=6 * D * H, transcendentals=n * T * H),
    )(x, dy, wg, wu, wd, a1, a2, df, d2)
    return ig, factor * first, factor * p2, factor * p1, factor * second


def solution(mesh):
    in_specs = (
        P(("dp", "tensor"), None),
        P(("dp", "tensor"), None),
        P(None, "tensor"),
        P(None, "tensor"),
        P("tensor", None),
        P(),
        P(None, None, "tensor"),
        P(None, "tensor"),
        P(),
    )
    out_specs = (P(("dp", "tensor"), None), P(), P(None, None, "tensor"), P(None, "tensor"), P())
    return jax.shard_map(shards, mesh=mesh, in_specs=in_specs, out_specs=out_specs, check_vma=False)
```

time: 165 us -> 166 us (level)
  local copies, waits for them, and re-layouts: 5.31 us -> 0.78 us
  other arithmetic: 1.8 us -> 6.25 us
    mul x2 -> x4, other arithmetic: 1.8 us -> 6.25 us  [shards(): return (ig, factor * first, factor * p2, factor * p1, factor * second)]
    transpose x2 -> x0, local copies, waits for them, and re-layouts: 1.85 us -> none  [shards(): first = g[:, :2 * R].transpose(0, 2, 1).reshape(D, 2 * R)]
where the time goes in v2:
time: 166 us; the launch traced here: 165 us
  Pallas kernels  158 us (95%)
  other arithmetic  6.25 us (4%)
    pallas_call x1, Pallas kernels, shards(): pl.pallas_call(functools.partial(kernel, n, m, T, H, R, TW, W, cp, cg), o...  158 us
    mul x4, other arithmetic, shards(): return (ig, factor * first, factor * p2, factor * p1, factor * second)  6.25 us

profile of v2, /device:TPU:0, one launch (start us, length us, event | category | flops | bytes accessed | tf_op | source)
XLA Modules:
  0.0 165.3 jit_solution(13157439089951411469)
XLA Ops:
  0.6 157.6 %shard_map.128 = (bf16[64,3584]{1,0:T(8,128)(2,1)}, f32[3584,128]{1,0:T(8,128)}, f32[64,3584]{1,0:T(8,128)}, f32[2,64,1280]{2,1,0:T(8,128)}, f32[64,1280]{1,0:T(8,128)}) custom-call(bf16[64,3584]{1,0:T(8,128)(2,1)} %x_ref.1, bf16[64,3584]{1,0:T(8,128)(2,1)} %dy_ref.1, bf16[3584,1280]{1,0:T(8,128)(2,1)} %wg_ref.1, bf16[3584,1280]{1,0:T(8,128)(2,1)} %wu_ref.1, ...), custom_call_target="tpu_custom_call" | custom-call | flops 23488102400 | bytes 27525120 | tf_op jit(solution)/shard_map/pallas_call | solution.py:432
  158.3 0.0 copy-start.1
  158.3 0.0 copy-start
  158.3 1.9 %broadcast_multiply_fusion.3 = f32[64,1280]{1,0:T(8,128)} fusion(f32[64,1280]{1,0:T(8,128)} %get-tuple-element.13), kind=kLoop, calls=%fused_computation.3 | loop fusion | flops 81920 | bytes 655360 | tf_op jit(solution)/shard_map/mul | solution.py:465
  160.2 2.0 %broadcast_multiply_fusion.2 = f32[2,64,1280]{2,1,0:T(8,128)} fusion(f32[2,64,1280]{2,1,0:T(8,128)} %get-tuple-element.12), kind=kLoop, calls=%fused_computation.2 | loop fusion | flops 163840 | bytes 1310720 | tf_op jit(solution)/shard_map/mul | solution.py:465
  162.2 0.0 copy-done.1
  162.2 1.0 broadcast_multiply_fusion.1
  163.2 0.0 copy-done
  163.2 0.0 copy-start.2
  163.2 1.4 broadcast_multiply_fusion
  164.6 0.0 copy-done.2
  164.6 0.8 copy.15
Async XLA Ops:
  158.3 3.9 %copy-start.1 = (f32[64,3584]{1,0:T(8,128)S(1)}, f32[64,3584]{1,0:T(8,128)}, u32[]{:S(2)}) copy-start(f32[64,3584]{1,0:T(8,128)} %get-tuple-element.14) | copy-start | bytes 2752516
  158.3 4.9 %copy-start = (f32[3584,128]{1,0:T(8,128)S(1)}, f32[3584,128]{1,0:T(8,128)}, u32[]{:S(2)}) copy-start(f32[3584,128]{1,0:T(8,128)} %get-tuple-element.11) | copy-start | bytes 5505028
  163.2 1.4 copy-start.2

commit v3 on v2

--- a/solution.py
+++ b/solution.py
@@ -205,30 +205,65 @@
     def die_copy(h, c):
         return send_to(term.at[h, c, 1 - core], die.at[h, c], die_s.at[h, c], die_r.at[h, c], {"tensor": partner})
 
-    def rs_copy(h, c, k, slot):
-        other = lax.rem(z + k, nz)
+    def rs_copy(h, c, b, slot, to):
         return send_to(
-            term.at[h, c, core, other], rsr.at[h, c, slot], rs_s.at[h, c, k], rs_r.at[h, c, slot],
-            {"tensor": 2 * other + core},
+            term.at[h, c, core, b], rsr.at[h, c, slot], rs_s.at[h, c, b], rs_r.at[h, c, slot], {"tensor": to}
         )
+
+    lower = lax.rem(t + n - 2, n)
+    upper = lax.rem(t + 2, n)
 
     def chip_sum(h, c):
         die_copy(h, c).wait_recv()
         term[h, c, core] = (term[h, c, core].astype(f32) + die[h, c].astype(f32)).astype(bf16)
-        for k in range(1, nz):
-            rs_copy(h, c, k, z).start()
-
-    def term_tile(h, c):
-        span = pl.ds(pl.multiple_of(c * W, W), W)
-        v = (dot_nt(dgate[...], wg[span, :]) + dot_nt(dup[...], wu[span, :])).astype(bf16)
-        v = v.reshape(nz, 2, S, W)
-        term[h, c, 0] = v[:, 0]
-        term[h, c, 1] = v[:, 1]
-        die_copy(h, c).start()
-
-        @pl.when(c > 0)
-        def _():
-            chip_sum(h, c - 1)
+
+    def take(h, c, b, slot, to):
+        rs_copy(h, c, b, slot, to).wait_recv()
+        term[h, c, core, b] = (term[h, c, core, b].astype(f32) + rsr[h, c, slot].astype(f32)).astype(bf16)
+
+    def downward(h, c):
+        @pl.when(z < nz - 1)
+        def _():
+            loop(0, z + 1, lambda b: take(h, c, b, b, upper))
+
+        loop(0, z, lambda b: rs_copy(h, c, b, b, lower).start())
+
+    def upward(h, c):
+        @pl.when(z > 0)
+        def _():
+            loop(z, nz, lambda b: take(h, c, b, b + 1, lower))
+
+        loop(z + 1, nz, lambda b: rs_copy(h, c, b, b + 1, upper).start())
+
+    NI = NC + nz
+
+    def term_step(h, i):
+        @pl.when(i < NC)
+        def _():
+            span = pl.ds(pl.multiple_of(i * W, W), W)
+            v = (dot_nt(dgate[...], wg[span, :]) + dot_nt(dup[...], wu[span, :])).astype(bf16)
+            v = v.reshape(nz, 2, S, W)
+            term[h, i, 0] = v[:, 0]
+            term[h, i, 1] = v[:, 1]
+            die_copy(h, i).start()
+
+        c = i - 1
+
+        @pl.when(jnp.logical_and(c >= 0, c < NC))
+        def _():
+            chip_sum(h, c)
+
+        cd = c - (nz - 1 - z)
+
+        @pl.when(jnp.logical_and(cd >= 0, cd < NC))
+        def _():
+            downward(h, cd)
+
+        cu = c - z
+
+        @pl.when(jnp.logical_and(cu >= 0, cu < NC))
+        def _():
+            upward(h, cu)
 
     loads[0].wait()
     forward(lines_x[0], 0, True)
@@ -260,16 +295,10 @@
     forward(lines_dy[1], 0, True)
     keep_low(0)
     input_rank(1)
-    per = -(-NC // (n - 1))
 
     def mixed(s):
         forward(lines_dy[1], s)
-        for i in range(per):
-            c = (s - 1) * per + i
-
-            @pl.when(c < NC)
-            def _():
-                term_tile(0, c)
+        term_step(0, s - 1)
 
         @pl.when(s - 1 < NT)
         def _():
@@ -277,10 +306,18 @@
 
     loop(1, n, mixed)
     loop(n - 1, NT, lambda j: forward_tile(1, j))
-    chip_sum(0, NC - 1)
 
     cotangent_rank(1)
-    loop(0, NT, lambda j: backward_tile(1, j))
+
+    def backward_beside(j):
+        backward_tile(1, j)
+
+        @pl.when(n - 1 + j < NI)
+        def _():
+            term_step(0, n - 1 + j)
+
+    loop(0, NT, backward_beside)
+    loop(n - 1 + NT, NI, lambda i: term_step(0, i))
     keep_low(1)
 
     loop(1, n, lambda k: low_copy(k, t).start())
@@ -292,8 +329,8 @@
             psend[q // cp, q % cp] = jnp.zeros((R, 128), bf16)
     loop(1, m, lambda k: p_copy(k, d).start())
 
-    cut1, cut2, cut3 = NC // 4, NC // 2, (3 * NC) // 4
-    loop(0, cut1, lambda c: term_tile(1, c))
+    cut1, cut2, cut3 = NI // 5, (2 * NI) // 5, (3 * NI) // 5
+    loop(0, cut1, lambda i: term_step(1, i))
 
     lowr[t] = lowb[t]
     loop(1, n, lambda k: low_copy(k, lax.rem(t + k, n)).wait_recv())
@@ -304,7 +341,7 @@
     ulow[t] = total.astype(bf16)
     loop(1, n, lambda k: ul_copy(k, t).start())
 
-    loop(cut1, cut2, lambda c: term_tile(1, c))
+    loop(cut1, cut2, lambda i: term_step(1, i))
 
     loop(1, n, lambda k: ul_copy(k, lax.rem(t + k, n)).wait_recv())
     u_t = [ulow[:, h].reshape(n * S, 3 * R).astype(f32).T.astype(bf16) for h in range(2)]
@@ -329,7 +366,7 @@
 
     loop(1, m, lambda k: g_copy(k, d).start())
 
-    loop(cut2, cut3, lambda c: term_tile(1, c))
+    loop(cut2, cut3, lambda i: term_step(1, i))
 
     precv[d] = psend[d]
     loop(1, m, lambda k: p_copy(k, other_d(k)).wait_recv())
@@ -339,8 +376,7 @@
     pfin[d] = total.astype(bf16)
     loop(1, m, lambda k: pf_copy(k, d).start())
 
-    loop(cut3, NC, lambda c: term_tile(1, c))
-    chip_sum(1, NC - 1)
+    loop(cut3, NI, lambda i: term_step(1, i))
 
     grecv[d] = gsend[d]
     loop(1, m, lambda k: g_copy(k, other_d(k)).wait_recv())
@@ -364,10 +400,6 @@
         span = pl.ds(pl.multiple_of(c * W, W), W)
         part = slice(h * S, (h + 1) * S)
         total = term[h, c, core, z].astype(f32) + adapter_scale * dot_nt(u_own[part, : 2 * R], a1_ref[span, :])
-        for k in range(1, nz):
-            other = lax.rem(z + k, nz)
-            rs_copy(h, c, k, other).wait_recv()
-            total = total + rsr[h, c, other].astype(f32)
         ig_ref[part, span] = total.astype(bf16)
 
     loop(0, NC, lambda c: finish(0, c))
@@ -403,8 +435,8 @@
     def sent(c):
         for h in range(2):
             die_copy(h, c).wait_send()
-            for k in range(1, nz):
-                rs_copy(h, c, k, z).wait_send()
+            loop(0, z, lambda b: rs_copy(h, c, b, b, lower).wait_send())
+            loop(z + 1, nz, lambda b: rs_copy(h, c, b, b + 1, upper).wait_send())
 
     loop(0, NC, sent)
 
@@ -418,7 +450,7 @@
     S = T // 2
     GH = n * S
     TW = 256 if H % 256 == 0 else 128
-    W = 256
+    W = 512 if D % 512 == 0 else 256
     NC = D // W
     cp = -(-3 * (H // 128) // m)
     cg = -(-3 * (D // 128) // (2 * m))
@@ -449,13 +481,13 @@
             V((n, 2, S, 3 * R), bf16), V((T, 3 * R), bf16),
             V((3, R, H), f32), V((m, cp, R, 128), bf16), V((m, cp, R, 128), bf16), V((m, cp, R, 128), bf16),
             V((m, cg, R, 128), bf16), V((m, cg, R, 128), bf16), V((2, m, cg, R, 128), bf16),
-            V((2, NC, 2, nz, S, W), bf16), V((2, NC, nz, S, W), bf16), V((2, NC, nz, S, W), bf16),
+            V((2, NC, 2, nz, S, W), bf16), V((2, NC, nz, S, W), bf16), V((2, NC, nz + 1, S, W), bf16),
             DMA((7,)),
             DMA((2, 2, n)), DMA((2, n)), DMA((2, 2, n)), DMA((2, n)),
             DMA((n,)), DMA((n,)), DMA((n,)), DMA((n,)),
             DMA((m,)), DMA((m,)), DMA((m,)), DMA((m,)),
             DMA((m,)), DMA((m,)), DMA((m,)), DMA((m,)), DMA((m,)), DMA((m,)),
-            DMA((2, NC)), DMA((2, NC)), DMA((2, NC, nz)), DMA((2, NC, nz)),
+            DMA((2, NC)), DMA((2, NC)), DMA((2, NC, nz)), DMA((2, NC, nz + 1)),
         ],
         compiler_params=pltpu.CompilerParams(
             collective_id=0, has_side_effects=True, vmem_limit_bytes=63 * 1024 * 1024

time: 166 us -> 169 us (1.018)
  Pallas kernels: 158 us -> 160 us
    pallas_call x1, Pallas kernels: 158 us -> 160 us  [shards(): pl.pallas_call(functools.partial(kernel, n, m, T, H, R, TW, W, cp, cg), o...]
where the time goes in v3:
time: 169 us; the launch traced here: 168 us
  Pallas kernels  160 us (95%)
  other arithmetic  6.25 us (4%)
    pallas_call x1, Pallas kernels, shards(): pl.pallas_call(functools.partial(kernel, n, m, T, H, R, TW, W, cp, cg), o...  160 us
    mul x4, other arithmetic, shards(): return (ig, factor * first, factor * p2, factor * p1, factor * second)  6.25 us

profile of v3, /device:TPU:0, one launch (start us, length us, event | category | flops | bytes accessed | tf_op | source)
XLA Modules:
  0.0 167.5 jit_solution(2857359552800347028)
XLA Ops:
  0.6 159.8 %shard_map.128 = (bf16[64,3584]{1,0:T(8,128)(2,1)}, f32[3584,128]{1,0:T(8,128)}, f32[64,3584]{1,0:T(8,128)}, f32[2,64,1280]{2,1,0:T(8,128)}, f32[64,1280]{1,0:T(8,128)}) custom-call(bf16[64,3584]{1,0:T(8,128)(2,1)} %x_ref.1, bf16[64,3584]{1,0:T(8,128)(2,1)} %dy_ref.1, bf16[3584,1280]{1,0:T(8,128)(2,1)} %wg_ref.1, bf16[3584,1280]{1,0:T(8,128)(2,1)} %wu_ref.1, ...), custom_call_target="tpu_custom_call" | custom-call | flops 23488102400 | bytes 27525120 | tf_op jit(solution)/shard_map/pallas_call | solution.py:464
  160.5 0.0 copy-start.1
  160.5 0.0 copy-start
  160.5 1.9 %broadcast_multiply_fusion.3 = f32[64,1280]{1,0:T(8,128)} fusion(f32[64,1280]{1,0:T(8,128)} %get-tuple-element.13), kind=kLoop, calls=%fused_computation.3 | loop fusion | flops 81920 | bytes 655360 | tf_op jit(solution)/shard_map/mul | solution.py:497
  162.4 2.0 %broadcast_multiply_fusion.2 = f32[2,64,1280]{2,1,0:T(8,128)} fusion(f32[2,64,1280]{2,1,0:T(8,128)} %get-tuple-element.12), kind=kLoop, calls=%fused_computation.2 | loop fusion | flops 163840 | bytes 1310720 | tf_op jit(solution)/shard_map/mul | solution.py:497
  164.3 0.0 copy-done.1
  164.3 1.0 broadcast_multiply_fusion.1
  165.3 0.0 copy-done
  165.3 0.0 copy-start.2
  165.3 1.4 broadcast_multiply_fusion
  166.7 0.0 copy-done.2
  166.7 0.8 copy.15
Async XLA Ops:
  160.5 3.9 %copy-start.1 = (f32[64,3584]{1,0:T(8,128)S(1)}, f32[64,3584]{1,0:T(8,128)}, u32[]{:S(2)}) copy-start(f32[64,3584]{1,0:T(8,128)} %get-tuple-element.14) | copy-start | bytes 2752516
  160.5 4.9 %copy-start = (f32[3584,128]{1,0:T(8,128)S(1)}, f32[3584,128]{1,0:T(8,128)}, u32[]{:S(2)}) copy-start(f32[3584,128]{1,0:T(8,128)} %get-tuple-element.11) | copy-start | bytes 5505028
  165.3 1.4 copy-start.2

commit v4 on v3

--- a/solution.py
+++ b/solution.py
@@ -28,7 +28,7 @@
     ig_ref, first_ref, second_ref, p2_ref, p1_ref,
     xg, dyg, wg, wu, wd, gate, up, dgate, dup,
     xlow, xlow_t, dylow, dylow_t, low, lowb, lowr, ulow, u_own,
-    pacc, psend, precv, pfin, gsend, grecv, gfin, term, die, rsr,
+    dhid, hid, ulow_t, pacc, psend, precv, pfin, gsend, grecv, gfin, term, die, rsr,
     load_sem, x_s, x_r, dy_s, dy_r, low_s, low_r, ul_s, ul_r,
     p_s, p_r, pf_s, pf_r, g_s, g_r, gf_s, gf_r, gd_s, gd_r, die_s, die_r, rs_s, rs_r,
 ):
@@ -42,6 +42,8 @@
     D = x_ref.shape[1]
     NC = D // W
     NT = H // TW
+    KC = W
+    NK = D // KC
     HC = H // 128
     DC = D // 128
 
@@ -127,38 +129,49 @@
         xlow[...] = xl.astype(bf16)
         xlow_t[...] = xl.T.astype(bf16)
 
-    def forward_tile(h, j):
-        cols = tile_cols(j)
-        gate[:, cols] = dot(xg[h], wg[:, cols]) + adapter_scale * dot(xlow[:, :R], a2_ref[0, :, cols])
-        up[:, cols] = dot(xg[h], wu[:, cols]) + adapter_scale * dot(xlow[:, R:], a2_ref[1, :, cols])
+    def depth(k):
+        return pl.ds(pl.multiple_of(k * KC, KC), KC)
+
+    def forward_start():
+        gate[...] = adapter_scale * dot(xlow[:, :R], a2_ref[0])
+        up[...] = adapter_scale * dot(xlow[:, R:], a2_ref[1])
+
+    def forward_part(h, k):
+        a = xg[h, :, depth(k)]
+        gate[...] += dot(a, wg[depth(k), :])
+        up[...] += dot(a, wu[depth(k), :])
 
     def cotangent_rank(h):
         dl = dot_nt(dyg[h], d2_ref[...])
         dylow[...] = dl.astype(bf16)
         dylow_t[...] = dl.T.astype(bf16)
-        low[...] = jnp.zeros_like(low)
-
-    def backward_tile(h, j):
+        dhid[...] = adapter_scale * dot(dylow[...], df_ref[...])
+
+    def backward_part(h, k):
+        dhid[...] += dot_nt(dyg[h, :, depth(k)], wd[:, depth(k)])
+
+    def pointwise(j):
         cols = tile_cols(j)
-        dh = dot_nt(dyg[h], wd[cols, :]) + adapter_scale * dot(dylow[...], df_ref[:, cols])
+        dh = dhid[:, cols]
         gp = gate[:, cols]
         u = up[:, cols]
         sig = jax.nn.sigmoid(gp)
         act = gp * sig
-        dg = (dh * u * sig * (1.0 + gp * (1.0 - sig))).astype(bf16)
-        du = (dh * act).astype(bf16)
-        hd = (act * u).astype(bf16)
-        dgate[:, cols] = dg
-        dup[:, cols] = du
-        for i, (a, b) in enumerate([(xlow_t[:R, :], dg), (xlow_t[R:, :], du), (dylow_t[...], hd)]):
-            v = dot(a, b)
+        dgate[:, cols] = (dh * u * sig * (1.0 + gp * (1.0 - sig))).astype(bf16)
+        dup[:, cols] = (dh * act).astype(bf16)
+        hid[:, cols] = (act * u).astype(bf16)
+
+    def rank_products(h):
+        for i, (a, b) in enumerate([(xlow_t[:R, :], dgate), (xlow_t[R:, :], dup), (dylow_t[...], hid)]):
+            v = dot(a, b[...])
             if h == 0:
-                pacc[i, :, cols] = v
+                pacc[i] = v
             else:
-                pacc[i, :, cols] += v
-        low[:, :R] += dot_nt(dg, a2_ref[0, :, cols])
-        low[:, R : 2 * R] += dot_nt(du, a2_ref[1, :, cols])
-        low[:, 2 * R :] += dot_nt(hd, df_ref[:, cols])
+                pacc[i] += v
+        low[:, :R] = dot_nt(dgate[...], a2_ref[0])
+        low[:, R : 2 * R] = dot_nt(dup[...], a2_ref[1])
+        low[:, 2 * R :] = dot_nt(hid[...], df_ref[...])
+        keep_low(h)
 
     def keep_low(h):
         lowb[:, h] = low[...].astype(bf16).reshape(n, S, 3 * R)
@@ -183,8 +196,12 @@
     def p_copy(k, slot):
         return scatter_copy(psend, precv, p_s, p_r, k, slot)
 
+    def g_part(e):
+        return pl.ds((core * m + e) * cg, cg)
+
     def g_copy(k, slot):
-        return scatter_copy(gsend, grecv, g_s, g_r, k, slot)
+        peer = lax.rem(d + k, m)
+        return send_to(gsend.at[g_part(peer)], grecv.at[slot], g_s.at[k], g_r.at[slot], {"dp": peer})
 
     def pf_copy(k, slot):
         peer = lax.rem(d + k, m)
@@ -271,54 +288,58 @@
     loads[1].wait()
     forward(lines_dy[0], 0, True)
     input_rank(0)
+    forward_start()
     loads[4].wait()
     loads[5].wait()
 
     def beside(line, s, h, tile):
         forward(line, s)
 
-        @pl.when(s - 1 < NT)
+        @pl.when(s - 1 < NK)
         def _():
             tile(h, s - 1)
 
-    loop(1, n, lambda s: beside(lines_dy[0], s, 0, forward_tile))
-    loop(n - 1, NT, lambda j: forward_tile(0, j))
+    loop(1, n, lambda s: beside(lines_dy[0], s, 0, forward_part))
+    loop(n - 1, NK, lambda j: forward_part(0, j))
 
     loads[2].wait()
     forward(lines_x[1], 0, True)
     cotangent_rank(0)
     loads[6].wait()
-    loop(1, n, lambda s: beside(lines_x[1], s, 0, backward_tile))
-    loop(n - 1, NT, lambda j: backward_tile(0, j))
+    loop(1, n, lambda s: beside(lines_x[1], s, 0, backward_part))
+    loop(n - 1, NK, lambda j: backward_part(0, j))
+    loop(0, NT, pointwise)
+    rank_products(0)
 
     loads[3].wait()
     forward(lines_dy[1], 0, True)
-    keep_low(0)
     input_rank(1)
+    forward_start()
 
     def mixed(s):
         forward(lines_dy[1], s)
         term_step(0, s - 1)
 
-        @pl.when(s - 1 < NT)
-        def _():
-            forward_tile(1, s - 1)
+        @pl.when(s - 1 < NK)
+        def _():
+            forward_part(1, s - 1)
 
     loop(1, n, mixed)
-    loop(n - 1, NT, lambda j: forward_tile(1, j))
+    loop(n - 1, NK, lambda j: forward_part(1, j))
 
     cotangent_rank(1)
 
     def backward_beside(j):
-        backward_tile(1, j)
+        backward_part(1, j)
 
         @pl.when(n - 1 + j < NI)
         def _():
             term_step(0, n - 1 + j)
 
-    loop(0, NT, backward_beside)
-    loop(n - 1 + NT, NI, lambda i: term_step(0, i))
-    keep_low(1)
+    loop(0, NK, backward_beside)
+    loop(n - 1 + NK, NI, lambda i: term_step(0, i))
+    loop(0, NT, pointwise)
+    rank_products(1)
 
     loop(1, n, lambda k: low_copy(k, t).start())
     for q in range(m * cp):
@@ -344,26 +365,22 @@
     loop(cut1, cut2, lambda i: term_step(1, i))
 
     loop(1, n, lambda k: ul_copy(k, lax.rem(t + k, n)).wait_recv())
-    u_t = [ulow[:, h].reshape(n * S, 3 * R).astype(f32).T.astype(bf16) for h in range(2)]
-    for q in range(2 * m * cg):
-        g, j = divmod(q, DC)
-        if q % (m * cg) == 0:
-            owner_side = q // (m * cg)
-        if g < 3:
-            src = xg if g < 2 else dyg
-
-            @pl.when(core == owner_side)
-            def _(q=q, g=g, j=j, src=src):
-                acc = 0.0
-                for h in range(2):
-                    acc = acc + dot(u_t[h][g * R : (g + 1) * R], src[h, :, 128 * j : 128 * (j + 1)])
-                gsend[(q // cg) % m, q % cg] = acc.astype(bf16)
-        else:
-
-            @pl.when(core == owner_side)
-            def _(q=q):
-                gsend[(q // cg) % m, q % cg] = jnp.zeros((R, 128), bf16)
-
+    for h in range(2):
+        ulow_t[h] = ulow[:, h].reshape(n * S, 3 * R).astype(f32).T.astype(bf16)
+    u_t = [ulow_t.at[h] for h in range(2)]
+    for q in range(3 * DC, 2 * m * cg):
+        gsend[q] = jnp.zeros((R, 128), bf16)
+
+    def factor_part(k):
+        for src, lo, hi in ((xg, 0, 2), (dyg, 2, 3)):
+            v = dot(u_t[0][lo * R : hi * R], src[0, :, depth(k)]) + dot(u_t[1][lo * R : hi * R], src[1, :, depth(k)])
+            for g in range(lo, hi):
+                for i in range(KC // 128):
+                    gsend[g * DC + k * (KC // 128) + i] = v[
+                        (g - lo) * R : (g - lo + 1) * R, 128 * i : 128 * (i + 1)
+                    ].astype(bf16)
+
+    loop(0, NK, factor_part)
     loop(1, m, lambda k: g_copy(k, d).start())
 
     loop(cut2, cut3, lambda i: term_step(1, i))
@@ -378,7 +395,7 @@
 
     loop(cut3, NI, lambda i: term_step(1, i))
 
-    grecv[d] = gsend[d]
+    grecv[d] = gsend[g_part(d)]
     loop(1, m, lambda k: g_copy(k, other_d(k)).wait_recv())
     total = grecv[0].astype(f32)
     for e in range(1, m):
@@ -479,8 +496,9 @@
             V((GH, 2 * R), bf16), V((2 * R, GH), bf16), V((GH, R), bf16), V((R, GH), bf16),
             V((GH, 3 * R), f32), V((n, 2, S, 3 * R), bf16), V((n, 2, S, 3 * R), bf16),
             V((n, 2, S, 3 * R), bf16), V((T, 3 * R), bf16),
+            V((GH, H), f32), V((GH, H), bf16), V((2, 3 * R, GH), bf16),
             V((3, R, H), f32), V((m, cp, R, 128), bf16), V((m, cp, R, 128), bf16), V((m, cp, R, 128), bf16),
-            V((m, cg, R, 128), bf16), V((m, cg, R, 128), bf16), V((2, m, cg, R, 128), bf16),
+            V((2 * m * cg, R, 128), bf16), V((m, cg, R, 128), bf16), V((2, m, cg, R, 128), bf16),
             V((2, NC, 2, nz, S, W), bf16), V((2, NC, nz, S, W), bf16), V((2, NC, nz + 1, S, W), bf16),
             DMA((7,)),
             DMA((2, 2, n)), DMA((2, n)), DMA((2, 2, n)), DMA((2, n)),

time: 169 us -> 175 us (1.036)
  Pallas kernels: 160 us -> 165 us
    pallas_call x1, Pallas kernels: 160 us -> 165 us  [shards(): pl.pallas_call(functools.partial(kernel, n, m, T, H, R, TW, W, cp, cg), o...]
where the time goes in v4:
time: 175 us; the launch traced here: 173 us
  Pallas kernels  165 us (94%)
  other arithmetic  6.25 us (4%)
    pallas_call x1, Pallas kernels, shards(): pl.pallas_call(functools.partial(kernel, n, m, T, H, R, TW, W, cp, cg), o...  165 us
    mul x4, other arithmetic, shards(): return (ig, factor * first, factor * p2, factor * p1, factor * second)  6.25 us

profile of v4, /device:TPU:0, one launch (start us, length us, event | category | flops | bytes accessed | tf_op | source)
XLA Modules:
  0.0 172.9 jit_solution(16424072010343708876)
XLA Ops:
  0.6 165.2 %shard_map.128 = (bf16[64,3584]{1,0:T(8,128)(2,1)}, f32[3584,128]{1,0:T(8,128)}, f32[64,3584]{1,0:T(8,128)}, f32[2,64,1280]{2,1,0:T(8,128)}, f32[64,1280]{1,0:T(8,128)}) custom-call(bf16[64,3584]{1,0:T(8,128)(2,1)} %x_ref.1, bf16[64,3584]{1,0:T(8,128)(2,1)} %dy_ref.1, bf16[3584,1280]{1,0:T(8,128)(2,1)} %wg_ref.1, bf16[3584,1280]{1,0:T(8,128)(2,1)} %wu_ref.1, ...), custom_call_target="tpu_custom_call" | custom-call | flops 23488102400 | bytes 27525120 | tf_op jit(solution)/shard_map/pallas_call | solution.py:481
  165.9 0.0 copy-start.1
  165.9 0.0 copy-start
  165.9 1.9 %broadcast_multiply_fusion.3 = f32[64,1280]{1,0:T(8,128)} fusion(f32[64,1280]{1,0:T(8,128)} %get-tuple-element.13), kind=kLoop, calls=%fused_computation.3 | loop fusion | flops 81920 | bytes 655360 | tf_op jit(solution)/shard_map/mul | solution.py:515
  167.8 2.0 %broadcast_multiply_fusion.2 = f32[2,64,1280]{2,1,0:T(8,128)} fusion(f32[2,64,1280]{2,1,0:T(8,128)} %get-tuple-element.12), kind=kLoop, calls=%fused_computation.2 | loop fusion | flops 163840 | bytes 1310720 | tf_op jit(solution)/shard_map/mul | solution.py:515
  169.7 0.0 copy-done.1
  169.7 1.0 broadcast_multiply_fusion.1
  170.8 0.0 copy-done
  170.8 0.0 copy-start.2
  170.8 1.4 broadcast_multiply_fusion
  172.1 0.0 copy-done.2
  172.1 0.8 copy.15
Async XLA Ops:
  165.9 3.9 %copy-start.1 = (f32[64,3584]{1,0:T(8,128)S(1)}, f32[64,3584]{1,0:T(8,128)}, u32[]{:S(2)}) copy-start(f32[64,3584]{1,0:T(8,128)} %get-tuple-element.14) | copy-start | bytes 2752516
  165.9 4.9 %copy-start = (f32[3584,128]{1,0:T(8,128)S(1)}, f32[3584,128]{1,0:T(8,128)}, u32[]{:S(2)}) copy-start(f32[3584,128]{1,0:T(8,128)} %get-tuple-element.11) | copy-start | bytes 5505028
  170.8 1.4 copy-start.2

commit v5 on v2

--- a/solution.py
+++ b/solution.py
@@ -71,50 +71,88 @@
         pl.semaphore_signal(barrier, inc=1, device_id={"dp": lax.rem(d + k, m)}, device_id_type=MESH)
     pl.semaphore_wait(barrier, n - 1 + m - 1)
 
-    right = lax.rem(t + 1, n)
-    left = lax.rem(t + n - 1, n)
+    toward = (lax.rem(t + 2, n), lax.rem(t + n - 2, n), partner)
 
     def hop(line, side, b):
         buf, s_sem, r_sem, h = line
         return pltpu.make_async_remote_copy(
             src_ref=buf.at[h, rows(b)], dst_ref=buf.at[h, rows(b)], send_sem=s_sem.at[h, side, b],
-            recv_sem=r_sem.at[h, b], device_id={"tensor": right if side == 0 else left}, device_id_type=MESH,
+            recv_sem=r_sem.at[h, b], device_id={"tensor": toward[side]}, device_id_type=MESH,
         )
 
-    def forward(line, s, first=False):
-        b = t - s
-
-        @pl.when(b >= 0)
-        def _():
-            if not first:
-                hop(line, 0, b).wait_recv()
-
-            @pl.when(t < n - 1)
+    def start(line):
+        @pl.when(z < nz - 1)
+        def _():
+            hop(line, 0, t).start()
+
+        @pl.when(z > 0)
+        def _():
+            hop(line, 1, t).start()
+
+        hop(line, 2, t).start()
+
+    def relay(line, s):
+        @pl.when(z >= s)
+        def _():
+            b = t - 2 * s
+            hop(line, 0, b).wait_recv()
+
+            @pl.when(z < nz - 1)
             def _():
                 hop(line, 0, b).start()
 
-        b2 = t + s
-
-        @pl.when(b2 < n)
-        def _():
-            if not first:
-                hop(line, 1, b2).wait_recv()
-
-            @pl.when(t > 0)
+            hop(line, 2, b).start()
+
+        @pl.when(z + s < nz)
+        def _():
+            b = t + 2 * s
+            hop(line, 1, b).wait_recv()
+
+            @pl.when(z > 0)
             def _():
-                hop(line, 1, b2).start()
+                hop(line, 1, b).start()
+
+            hop(line, 2, b).start()
+
+    def collect(line, s):
+        @pl.when(z >= s)
+        def _():
+            hop(line, 2, partner - 2 * s).wait_recv()
+
+        @pl.when(jnp.logical_and(z + s < nz, s > 0))
+        def _():
+            hop(line, 2, partner + 2 * s).wait_recv()
+
+    def forward(line, i):
+        odd = lax.rem(i, 2) == 1
+
+        @pl.when(jnp.logical_and(odd, i < n - 1))
+        def _():
+            relay(line, lax.div(i + 1, 2))
+
+        @pl.when(lax.rem(i, 2) == 0)
+        def _():
+            collect(line, lax.div(i, 2))
+
+        @pl.when(i == n - 1)
+        def _():
+            collect(line, 0)
 
     def drain(line):
-        def body(b):
-            @pl.when(jnp.logical_and(b <= t, t < n - 1))
+        def body(zb):
+            b = 2 * zb + core
+
+            @pl.when(jnp.logical_and(zb <= z, z < nz - 1))
             def _():
                 hop(line, 0, b).wait_send()
 
-            @pl.when(jnp.logical_and(b >= t, t > 0))
+            @pl.when(jnp.logical_and(zb >= z, z > 0))
             def _():
                 hop(line, 1, b).wait_send()
 
-        loop(0, n, body)
+            hop(line, 2, b).wait_send()
+
+        loop(0, nz, body)
 
     lines_x = [(xg, x_s, x_r, h) for h in range(2)]
     lines_dy = [(dyg, dy_s, dy_r, h) for h in range(2)]
@@ -231,10 +269,10 @@
             chip_sum(h, c - 1)
 
     loads[0].wait()
-    forward(lines_x[0], 0, True)
+    start(lines_x[0])
     loop(1, n, lambda s: forward(lines_x[0], s))
     loads[1].wait()
-    forward(lines_dy[0], 0, True)
+    start(lines_dy[0])
     input_rank(0)
     loads[4].wait()
     loads[5].wait()
@@ -250,14 +288,14 @@
     loop(n - 1, NT, lambda j: forward_tile(0, j))
 
     loads[2].wait()
-    forward(lines_x[1], 0, True)
+    start(lines_x[1])
     cotangent_rank(0)
     loads[6].wait()
     loop(1, n, lambda s: beside(lines_x[1], s, 0, backward_tile))
     loop(n - 1, NT, lambda j: backward_tile(0, j))
 
     loads[3].wait()
-    forward(lines_dy[1], 0, True)
+    start(lines_dy[1])
     keep_low(0)
     input_rank(1)
     per = -(-NC // (n - 1))
@@ -451,7 +489,7 @@
             V((m, cg, R, 128), bf16), V((m, cg, R, 128), bf16), V((2, m, cg, R, 128), bf16),
             V((2, NC, 2, nz, S, W), bf16), V((2, NC, nz, S, W), bf16), V((2, NC, nz, S, W), bf16),
             DMA((7,)),
-            DMA((2, 2, n)), DMA((2, n)), DMA((2, 2, n)), DMA((2, n)),
+            DMA((2, 3, n)), DMA((2, n)), DMA((2, 3, n)), DMA((2, n)),
             DMA((n,)), DMA((n,)), DMA((n,)), DMA((n,)),
             DMA((m,)), DMA((m,)), DMA((m,)), DMA((m,)),
             DMA((m,)), DMA((m,)), DMA((m,)), DMA((m,)), DMA((m,)), DMA((m,)),

time: 166 us -> 166 us (level)
  no operation moved by 1% of the time
where the time goes in v5:
time: 166 us
  Pallas kernels  158 us (95%)
  other arithmetic  6.25 us (4%)
    pallas_call x1, Pallas kernels, shards(): pl.pallas_call(functools.partial(kernel, n, m, T, H, R, TW, W, cp, cg), o...  158 us
    mul x4, other arithmetic, shards(): return (ig, factor * first, factor * p2, factor * p1, factor * second)  6.25 us

profile of v5, /device:TPU:0, one launch (start us, length us, event | category | flops | bytes accessed | tf_op | source)
XLA Modules:
  0.0 165.6 jit_solution(6660605404876569337)
XLA Ops:
  0.6 157.9 %shard_map.128 = (bf16[64,3584]{1,0:T(8,128)(2,1)}, f32[3584,128]{1,0:T(8,128)}, f32[64,3584]{1,0:T(8,128)}, f32[2,64,1280]{2,1,0:T(8,128)}, f32[64,1280]{1,0:T(8,128)}) custom-call(bf16[64,3584]{1,0:T(8,128)(2,1)} %x_ref.1, bf16[64,3584]{1,0:T(8,128)(2,1)} %dy_ref.1, bf16[3584,1280]{1,0:T(8,128)(2,1)} %wg_ref.1, bf16[3584,1280]{1,0:T(8,128)(2,1)} %wu_ref.1, ...), custom_call_target="tpu_custom_call" | custom-call | flops 23488102400 | bytes 27525120 | tf_op jit(solution)/shard_map/pallas_call | solution.py:470
  158.6 0.0 copy-start.1
  158.6 0.0 copy-start
  158.6 1.9 %broadcast_multiply_fusion.3 = f32[64,1280]{1,0:T(8,128)} fusion(f32[64,1280]{1,0:T(8,128)} %get-tuple-element.13), kind=kLoop, calls=%fused_computation.3 | loop fusion | flops 81920 | bytes 655360 | tf_op jit(solution)/shard_map/mul | solution.py:503
  160.5 2.0 %broadcast_multiply_fusion.2 = f32[2,64,1280]{2,1,0:T(8,128)} fusion(f32[2,64,1280]{2,1,0:T(8,128)} %get-tuple-element.12), kind=kLoop, calls=%fused_computation.2 | loop fusion | flops 163840 | bytes 1310720 | tf_op jit(solution)/shard_map/mul | solution.py:503
  162.4 0.0 copy-done.1
  162.4 1.0 broadcast_multiply_fusion.1
  163.4 0.0 copy-done
  163.4 0.0 copy-start.2
  163.4 1.4 broadcast_multiply_fusion
  164.8 0.0 copy-done.2
  164.8 0.8 copy.15
Async XLA Ops:
  158.6 3.9 %copy-start.1 = (f32[64,3584]{1,0:T(8,128)S(1)}, f32[64,3584]{1,0:T(8,128)}, u32[]{:S(2)}) copy-start(f32[64,3584]{1,0:T(8,128)} %get-tuple-element.14) | copy-start | bytes 2752516
  158.6 4.9 %copy-start = (f32[3584,128]{1,0:T(8,128)S(1)}, f32[3584,128]{1,0:T(8,128)}, u32[]{:S(2)}) copy-start(f32[3584,128]{1,0:T(8,128)} %get-tuple-element.11) | copy-start | bytes 5505028
  163.4 1.4 copy-start.2
